TPU v7x, 512 devices: a whole 4x8x8 slice. The times are simulated.
512 devices in a mesh: cannon: 128 (over z_hi, x, y), rep: 4 (over z_lo, core).
Axes of the slice: x: 4, y: 8, z: 8 (z_hi: 4, z_lo: 2; z = z_hi * 2 + z_lo), core: 2. Of those that a mesh axis runs over, the one named last changes fastest.
Arguments:
- root_margin: bfloat16 [512, 8, 128, 128], P('cannon', 'rep'), may hold values from -2.5 to 2.5
- inverse_root: bfloat16 [512, 8, 128, 128], P('cannon', 'rep'), may hold values from -2.5 to 2.5
- hamiltonian: bfloat16 [512, 8, 128, 128], P('cannon', 'rep'), may hold values from -0.25 to 0.25
- margin_mask: int32 [512, 8], P('cannon', 'rep'), may hold values from 0 to 1, as said below
- hamilton_mask: int32 [512, 8], P('cannon', 'rep'), may hold values from 0 to 1, as said below
Outputs:
- root_next: bfloat16 [512, 8, 128, 128], P('cannon', 'rep')
- inverse_next: bfloat16 [512, 8, 128, 128], P('cannon', 'rep')
- lowdin_product: bfloat16 [512, 8, 128, 128], P('cannon', 'rep')
Inputs may be any that keep to these rules, and one draw needn't show every extreme that they name: `margin_mask`: 0 or 1; slot 8 // 2 (the diagonal block) is 1 in every block row; all block rows of one index of cannon share a fill level drawn from the seed, from one eighth to full. `hamilton_mask`: 0 or 1; slot 8 // 2 (the diagonal block) is 1 in every block row; all block rows of one index of cannon share a fill level drawn from the seed, from one eighth to full.
All inputs are finite; a program needn't handle non-finite values.
Results may differ from a plain program's by a relative error of at most 0.018.
Values may be sent and summed in bfloat16 or wider, within the bound.
A program may use at most 64 MiB of HBM per device.

v0:
```python
import jax
import jax.numpy as jnp
from jax import lax
from jax.sharding import PartitionSpec as P


def from_behind(block, axis, distance):
    devices = range(lax.axis_size(axis))
    route = [((i - distance) % len(devices), i) for i in devices]
    return lax.ppermute(block, axis, route)


def side_by_side(arrays, axis, split_dim, concat_dim, along):
    both = jnp.concatenate(arrays, axis=along)
    filled, at, finished = (
        lax.all_to_all(both, axis, split_axis=split_dim, concat_axis=concat_dim, tiled=True),
        0,
        [],
    )
    for a in arrays:
        finished.append(lax.slice_in_dim(filled, at, at + a.shape[along], axis=along))
        at += a.shape[along]
    return tuple(finished)


def row_product(first_factor, second_factor, first_mask, pattern):
    rows_local = first_factor.shape[0]
    slot_count = first_factor.shape[1]
    block_size = first_factor.shape[2]
    half_band = slot_count // 2
    groups = lax.axis_size("rep")
    group_slots = slot_count // groups
    steps_needed = (half_band + rows_local - 1) // rows_local
    below = []
    above = []
    for distance in range(1, steps_needed + 1):
        count = min(rows_local, half_band - (distance - 1) * rows_local)
        below.insert(0, from_behind(second_factor, ("cannon", "rep"), distance))
        above.append(from_behind(second_factor, ("cannon", "rep"), -distance))
    extended = jnp.concatenate(below + [second_factor] + above, axis=0)
    summed = jnp.zeros((rows_local, slot_count, block_size, block_size), jnp.float32)
    for group in range(groups):
        partial_value = jnp.zeros((rows_local, slot_count, block_size, block_size), jnp.float32)
        for offset in range(group * group_slots, (group + 1) * group_slots):
            low_slot = max(0, offset - half_band)
            high_slot = min(slot_count, offset + half_band)
            window = extended[
                offset : offset + rows_local,
                low_slot - offset + half_band : high_slot - offset + half_band,
            ]
            present = jnp.any(first_mask[:, offset] > 0)
            factor_block = first_factor[:, offset]
            addend_shape = (rows_local, high_slot - low_slot, block_size, block_size)

            def compute_slot(factor_block=factor_block, window=window):
                return jnp.einsum(
                    "ipq,itqr->itpr", factor_block, window, preferred_element_type=jnp.float32
                )

            def skip_slot(addend_shape=addend_shape):
                return jnp.zeros(addend_shape, jnp.float32)

            partial_value = partial_value.at[:, low_slot:high_slot].add(
                lax.cond(present, compute_slot, skip_slot)
            )
        summed = summed + lax.optimization_barrier(partial_value.astype(jnp.bfloat16)).astype(
            jnp.float32
        )
    return summed * pattern[:, :, None, None].astype(jnp.float32)


def iterate(
    root_margin,
    inverse_root,
    hamiltonian,
    margin_mask,
    hamilton_mask,
    product_fn,
    slot_ids,
    slot_count,
):
    margin_scale = margin_mask[:, :, None, None].astype(jnp.bfloat16)
    hamilton_scale = hamilton_mask[:, :, None, None].astype(jnp.bfloat16)
    root_masked = root_margin * margin_scale
    inverse_masked = inverse_root * margin_scale
    hamilton_masked = hamiltonian * hamilton_scale
    product = product_fn(inverse_masked, root_masked, margin_mask, margin_mask)
    block_size = root_margin.shape[2]
    diagonal = (slot_ids == slot_count // 2).astype(jnp.float32)[None, :, None, None] * jnp.eye(
        block_size, dtype=jnp.float32
    )[None, None]
    polynomial = (1.5 * diagonal - 0.5 * product).astype(jnp.bfloat16)
    inverse_next = product_fn(polynomial, inverse_masked, margin_mask, margin_mask).astype(
        jnp.bfloat16
    )
    root_next = product_fn(root_masked, polynomial, margin_mask, margin_mask).astype(jnp.bfloat16)
    lowdin_product = product_fn(inverse_next, hamilton_masked, margin_mask, hamilton_mask).astype(
        jnp.bfloat16
    )
    return (root_next, inverse_next, lowdin_product)


def body(root_margin, inverse_root, hamiltonian, margin_mask, hamilton_mask):
    group_slots = root_margin.shape[1]
    slot_count = group_slots * lax.axis_size("rep")
    root_rows, inverse_rows, hamilton_rows, margin_rows, hamilton_rows_mask = (
        *side_by_side((root_margin, inverse_root, hamiltonian), "rep", 0, 1, 2),
        lax.all_to_all(margin_mask, "rep", split_axis=0, concat_axis=1, tiled=True),
        lax.all_to_all(hamilton_mask, "rep", split_axis=0, concat_axis=1, tiled=True),
    )
    slot_ids = jnp.arange(slot_count)
    root_next, inverse_next, lowdin_product = iterate(
        root_rows,
        inverse_rows,
        hamilton_rows,
        margin_rows,
        hamilton_rows_mask,
        row_product,
        slot_ids,
        slot_count,
    )
    return side_by_side((root_next, inverse_next, lowdin_product), "rep", 1, 0, 2)


def solution(mesh):
    in_specs = (
        P("cannon", "rep", None, None),
        P("cannon", "rep", None, None),
        P("cannon", "rep", None, None),
        P("cannon", "rep"),
        P("cannon", "rep"),
    )
    out_specs = (
        P("cannon", "rep", None, None),
        P("cannon", "rep", None, None),
        P("cannon", "rep", None, None),
    )
    return jax.shard_map(body, mesh=mesh, in_specs=in_specs, out_specs=out_specs, check_vma=False)
```

profile of v0, /device:TPU:1, one launch (start us, length us, event | category | flops | bytes accessed | tf_op | source)
XLA Modules:
  0.0 233.0 jit_solution(10943466908531655909)
XLA Ops:
  2.0 10.1 %all-to-all-start = ((s32[4,1,2]{2,1,0:T(1,128)}), s32[4,1,2]{2,1,0:T(1,128)S(1)}, u32[]{:S(2)}, u32[]{:S(2)}) async-start(s32[4,1,2]{2,1,0:T(1,128)} %copy.162), calls=%async_computation | async-start | bytes 4096 | tf_op jit(solution)/shard_map/all_to_all | solution.py:108
  15.0 6.1 %all_to_all.53 = s32[4,1,2]{2,1,0:T(1,128)S(1)} all-to-all(s32[4,1,2]{2,1,0:T(1,128)S(1)} %copy.232), channel_id=1, replica_groups=mesh['cannon'=128,'rep'=4] {'rep'}, dimensions={0} | all-to-all | bytes 64 | tf_op jit(solution)/shard_map/all_to_all | solution.py:109
  21.1 4.2 %all-to-all-start.1 = ((bf16[4,2,384,128]{3,2,1,0:T(8,128)(2,1)}), bf16[4,2,384,128]{3,2,1,0:T(8,128)(2,1)S(1)}, u32[]{:S(2)}, u32[]{:S(2)}) async-start(bf16[4,2,384,128]{3,2,1,0:T(8,128)(2,1)} %pad_maximum_fusion), calls=%async_computation.1 | async-start | bytes 1572864 | tf_op jit(solution)/shard_map/all_to_all | solution.py:16
  25.5 10.6 %all-to-all-done.1 = bf16[4,2,384,128]{3,2,1,0:T(8,128)(2,1)S(1)} async-done(((bf16[4,2,384,128]{3,2,1,0:T(8,128)(2,1)}), bf16[4,2,384,128]{3,2,1,0:T(8,128)(2,1)S(1)}, u32[]{:S(2)}, u32[]{:S(2)}) %all-to-all-start.1) | async-done | bytes 786464 | tf_op jit(solution)/shard_map/all_to_all | solution.py:16
  36.5 2.8 %collective-permute-start.4 = (bf16[1,8,128,128]{2,3,1,0:T(8,128)(2,1)S(1)}, bf16[1,8,128,128]{2,3,1,0:T(8,128)(2,1)S(1)}, u32[]{:S(2)}, u32[]{:S(2)}) collective-permute-start(bf16[1,8,128,128]{2,3,1,0:T(8,128)(2,1)S(1)} %get-tuple-element.1003), channel_id=1, source_target_pairs={{1,0},{2,1},{3,2},{4,3},{5,4},{6,5},{7,6},{8,7},{9,8},{10,9},{11,1... | collective-permute-start | bytes 786440 | tf_op jit(solution)/shard_map/ppermute | solution.py:10
  40.6 9.3 %collective-permute-start.5 = (bf16[1,8,128,128]{2,3,1,0:T(8,128)(2,1)S(1)}, bf16[1,8,128,128]{2,3,1,0:T(8,128)(2,1)S(1)}, u32[]{:S(2)}, u32[]{:S(2)}) collective-permute-start(bf16[1,8,128,128]{2,3,1,0:T(8,128)(2,1)S(1)} %get-tuple-element.1003), channel_id=1, source_target_pairs={{2,0},{3,1},{4,2},{5,3},{6,4},{7,5},{8,6},{9,7},{10,8},{11,9},{12,... | collective-permute-start | bytes 786440 | tf_op jit(solution)/shard_map/ppermute | solution.py:10
  49.9 4.1 %collective-permute-start.6 = (bf16[1,8,128,128]{2,3,1,0:T(8,128)(2,1)S(1)}, bf16[1,8,128,128]{2,3,1,0:T(8,128)(2,1)}, u32[]{:S(2)}, u32[]{:S(2)}) collective-permute-start(bf16[1,8,128,128]{2,3,1,0:T(8,128)(2,1)S(1)} %get-tuple-element.1003), channel_id=1, source_target_pairs={{3,0},{4,1},{5,2},{6,3},{7,4},{8,5},{9,6},{10,7},{11,8},{12,9},{13... | collective-permute-start | bytes 786440 | tf_op jit(solution)/shard_map/ppermute | solution.py:10
  60.0 2.2 collective-permute-start.2
  62.2 2.6 %collective-permute-start.3 = (bf16[1,8,128,128]{2,3,1,0:T(8,128)(2,1)S(1)}, bf16[1,8,128,128]{2,3,1,0:T(8,128)(2,1)S(1)}, u32[]{:S(2)}, u32[]{:S(2)}) collective-permute-start(bf16[1,8,128,128]{2,3,1,0:T(8,128)(2,1)S(1)} %get-tuple-element.1003), channel_id=1, source_target_pairs={{511,0},{0,1},{1,2},{2,3},{3,4},{4,5},{5,6},{6,7},{7,8},{8,9},{9,1... | collective-permute-start | bytes 786440 | tf_op jit(solution)/shard_map/ppermute | solution.py:10
  64.8 2.5 %conditional.36 = (f32[1,8,128,128]{3,2,0,1:T(8,128)}, f32[1,7,128,128]{3,2,0,1:T(8,128)S(1)}) conditional(s32[]{:T(128)} %bitcast.182, () %tuple.389, (bf16[1,8,128,128]{2,3,1,0:T(8,128)(2,1)S(1)}, bf16[1,8,128,128]{2,3,1,0:T(8,128)(2,1)S(1)}) %tuple.390), branch_computations={%region_8.0_spmd, %region_9.0_spmd} | conditional | flops 33554432 | bytes 3309584 | solution.py:64
  72.7 9.7 %collective-permute-start.19 = (bf16[1,8,128,128]{2,3,1,0:T(8,128)(2,1)S(1)}, bf16[1,8,128,128]{2,3,1,0:T(8,128)(2,1)}, u32[]{:S(2)}, u32[]{:S(2)}) collective-permute-start(bf16[1,8,128,128]{2,3,1,0:T(8,128)(2,1)S(1)} %get-tuple-element.1004), channel_id=1, source_target_pairs={{2,0},{3,1},{4,2},{5,3},{6,4},{7,5},{8,6},{9,7},{10,8},{11,9},{12,... | collective-permute-start | bytes 786440 | tf_op jit(solution)/shard_map/ppermute | solution.py:10
  86.8 3.5 %collective-permute-start.18 = (bf16[1,8,128,128]{2,3,1,0:T(8,128)(2,1)S(1)}, bf16[1,8,128,128]{2,3,1,0:T(8,128)(2,1)S(1)}, u32[]{:S(2)}, u32[]{:S(2)}) collective-permute-start(bf16[1,8,128,128]{2,3,1,0:T(8,128)(2,1)S(1)} %get-tuple-element.1004), channel_id=1, source_target_pairs={{1,0},{2,1},{3,2},{4,3},{5,4},{6,5},{7,6},{8,7},{9,8},{10,9},{11,1... | collective-permute-start | bytes 786440 | tf_op jit(solution)/shard_map/ppermute | solution.py:10
  90.4 3.3 %collective-permute-start.16 = (bf16[1,8,128,128]{2,3,1,0:T(8,128)(2,1)S(1)}, bf16[1,8,128,128]{2,3,1,0:T(8,128)(2,1)}, u32[]{:S(2)}, u32[]{:S(2)}) collective-permute-start(bf16[1,8,128,128]{2,3,1,0:T(8,128)(2,1)S(1)} %get-tuple-element.1004), channel_id=1, source_target_pairs={{510,0},{511,1},{0,2},{1,3},{2,4},{3,5},{4,6},{5,7},{6,8},{7,9},{8... | collective-permute-start | bytes 786440 | tf_op jit(solution)/shard_map/ppermute | solution.py:10
  93.7 2.3 %conditional.32 = (bf16[1,8,128,128]{3,2,0,1:T(8,128)(2,1)}, f32[1,5,128,128]{3,2,0,1:T(8,128)S(1)}) conditional(s32[]{:T(128)} %bitcast.177, () %tuple.381, (bf16[1,8,128,128]{2,3,1,0:T(8,128)(2,1)}, bf16[1,8,128,128]{2,3,1,0:T(8,128)(2,1)S(1)}) %tuple.382), branch_computations={%region_0.0_spmd, %region_1.0_spmd} | conditional | flops 16777216 | bytes 2981906 | solution.py:64
  96.1 2.5 %collective-permute-done.1 = bf16[1,8,128,128]{2,3,1,0:T(8,128)(2,1)} collective-permute-done((bf16[1,8,128,128]{2,3,1,0:T(8,128)(2,1)S(1)}, bf16[1,8,128,128]{2,3,1,0:T(8,128)(2,1)}, u32[]{:S(2)}, u32[]{:S(2)}) %collective-permute-start.1) | collective-permute-done | bytes 262176 | tf_op jit(solution)/shard_map/ppermute | solution.py:10
  98.6 3.4 %collective-permute-start.17 = (bf16[1,8,128,128]{2,3,1,0:T(8,128)(2,1)S(1)}, bf16[1,8,128,128]{2,3,1,0:T(8,128)(2,1)S(1)}, u32[]{:S(2)}, u32[]{:S(2)}) collective-permute-start(bf16[1,8,128,128]{2,3,1,0:T(8,128)(2,1)S(1)} %get-tuple-element.1004), channel_id=1, source_target_pairs={{511,0},{0,1},{1,2},{2,3},{3,4},{4,5},{5,6},{6,7},{7,8},{8,9},{9,1... | collective-permute-start | bytes 786440 | tf_op jit(solution)/shard_map/ppermute | solution.py:10
  105.1 2.3 conditional.52
  113.8 9.0 %collective-permute-start.26 = (bf16[1,8,128,128]{2,3,1,0:T(8,128)(2,1)S(1)}, bf16[1,8,128,128]{2,3,1,0:T(8,128)(2,1)}, u32[]{:S(2)}, u32[]{:S(2)}) collective-permute-start(bf16[1,8,128,128]{2,3,1,0:T(8,128)(2,1)S(1)} %get-tuple-element.1008), channel_id=1, source_target_pairs={{2,0},{3,1},{4,2},{5,3},{6,4},{7,5},{8,6},{9,7},{10,8},{11,9},{12,... | collective-permute-start | bytes 786440 | tf_op jit(solution)/shard_map/ppermute | solution.py:10
  123.0 2.6 %collective-permute-start.12 = (bf16[1,8,128,128]{3,2,0,1:T(8,128)(2,1)S(1)}, bf16[1,8,128,128]{3,2,0,1:T(8,128)(2,1)S(1)}, u32[]{:S(2)}, u32[]{:S(2)}) collective-permute-start(bf16[1,8,128,128]{3,2,0,1:T(8,128)(2,1)S(1)} %subtract_convert_fusion), channel_id=1, source_target_pairs={{2,0},{3,1},{4,2},{5,3},{6,4},{7,5},{8,6},{9,7},{10,8},{11,9},{12,... | collective-permute-start | bytes 786440 | tf_op jit(solution)/shard_map/ppermute | solution.py:10
  127.0 2.5 %collective-permute-start.11 = (bf16[1,8,128,128]{3,2,0,1:T(8,128)(2,1)S(1)}, bf16[1,8,128,128]{3,2,0,1:T(8,128)(2,1)}, u32[]{:S(2)}, u32[]{:S(2)}) collective-permute-start(bf16[1,8,128,128]{3,2,0,1:T(8,128)(2,1)S(1)} %subtract_convert_fusion), channel_id=1, source_target_pairs={{1,0},{2,1},{3,2},{4,3},{5,4},{6,5},{7,6},{8,7},{9,8},{10,9},{11,1... | collective-permute-start | bytes 786440 | tf_op jit(solution)/shard_map/ppermute | solution.py:10
  130.9 3.9 %collective-permute-start.13 = (bf16[1,8,128,128]{3,2,0,1:T(8,128)(2,1)S(1)}, bf16[1,8,128,128]{3,2,0,1:T(8,128)(2,1)S(1)}, u32[]{:S(2)}, u32[]{:S(2)}) collective-permute-start(bf16[1,8,128,128]{3,2,0,1:T(8,128)(2,1)S(1)} %subtract_convert_fusion), channel_id=1, source_target_pairs={{3,0},{4,1},{5,2},{6,3},{7,4},{8,5},{9,6},{10,7},{11,8},{12,9},{13... | collective-permute-start | bytes 786440 | tf_op jit(solution)/shard_map/ppermute | solution.py:10
  136.9 2.9 %collective-permute-start.9 = (bf16[1,8,128,128]{3,2,0,1:T(8,128)(2,1)S(1)}, bf16[1,8,128,128]{3,2,0,1:T(8,128)(2,1)S(1)}, u32[]{:S(2)}, u32[]{:S(2)}) collective-permute-start(bf16[1,8,128,128]{3,2,0,1:T(8,128)(2,1)S(1)} %subtract_convert_fusion), channel_id=1, source_target_pairs={{510,0},{511,1},{0,2},{1,3},{2,4},{3,5},{4,6},{5,7},{6,8},{7,9},{8... | collective-permute-start | bytes 786440 | tf_op jit(solution)/shard_map/ppermute | solution.py:10
  141.7 2.5 %conditional.44 = (f32[1,8,128,128]{3,2,0,1:T(8,128)}, f32[1,7,128,128]{3,2,0,1:T(8,128)S(1)}) conditional(s32[]{:T(128)} %bitcast.182, () %tuple.404, (bf16[1,8,128,128]{3,2,0,1:T(8,128)(2,1)S(1)}, bf16[1,8,128,128]{2,3,1,0:T(8,128)(2,1)S(1)}) %tuple.405), branch_computations={%region_24.0_spmd, %region_25.0_spmd} | conditional | flops 33554432 | bytes 3309584 | solution.py:64
  144.3 3.0 %collective-permute-done.11 = bf16[1,8,128,128]{3,2,0,1:T(8,128)(2,1)} collective-permute-done((bf16[1,8,128,128]{3,2,0,1:T(8,128)(2,1)S(1)}, bf16[1,8,128,128]{3,2,0,1:T(8,128)(2,1)}, u32[]{:S(2)}, u32[]{:S(2)}) %collective-permute-start.11) | collective-permute-done | bytes 262176 | tf_op jit(solution)/shard_map/ppermute | solution.py:10
  156.8 9.3 %collective-permute-start.27 = (bf16[1,8,128,128]{2,3,1,0:T(8,128)(2,1)S(1)}, bf16[1,8,128,128]{2,3,1,0:T(8,128)(2,1)}, u32[]{:S(2)}, u32[]{:S(2)}) collective-permute-start(bf16[1,8,128,128]{2,3,1,0:T(8,128)(2,1)S(1)} %get-tuple-element.1008), channel_id=1, source_target_pairs={{3,0},{4,1},{5,2},{6,3},{7,4},{8,5},{9,6},{10,7},{11,8},{12,9},{13... | collective-permute-start | bytes 786440 | tf_op jit(solution)/shard_map/ppermute | solution.py:10
  167.2 4.0 %collective-permute-start.25 = (bf16[1,8,128,128]{2,3,1,0:T(8,128)(2,1)S(1)}, bf16[1,8,128,128]{2,3,1,0:T(8,128)(2,1)}, u32[]{:S(2)}, u32[]{:S(2)}) collective-permute-start(bf16[1,8,128,128]{2,3,1,0:T(8,128)(2,1)S(1)} %get-tuple-element.1008), channel_id=1, source_target_pairs={{1,0},{2,1},{3,2},{4,3},{5,4},{6,5},{7,6},{8,7},{9,8},{10,9},{11,1... | collective-permute-start | bytes 786440 | tf_op jit(solution)/shard_map/ppermute | solution.py:10
  171.4 2.8 %collective-permute-start.23 = (bf16[1,8,128,128]{2,3,1,0:T(8,128)(2,1)S(1)}, bf16[1,8,128,128]{2,3,1,0:T(8,128)(2,1)}, u32[]{:S(2)}, u32[]{:S(2)}) collective-permute-start(bf16[1,8,128,128]{2,3,1,0:T(8,128)(2,1)S(1)} %get-tuple-element.1008), channel_id=1, source_target_pairs={{510,0},{511,1},{0,2},{1,3},{2,4},{3,5},{4,6},{5,7},{6,8},{7,9},{8... | collective-permute-start | bytes 786440 | tf_op jit(solution)/shard_map/ppermute | solution.py:10
  176.1 2.6 %collective-permute-done.8 = bf16[1,8,128,128]{3,2,0,1:T(8,128)(2,1)} collective-permute-done((bf16[1,8,128,128]{3,2,0,1:T(8,128)(2,1)S(1)}, bf16[1,8,128,128]{3,2,0,1:T(8,128)(2,1)}, u32[]{:S(2)}, u32[]{:S(2)}) %collective-permute-start.8) | collective-permute-done | bytes 262176 | tf_op jit(solution)/shard_map/ppermute | solution.py:10
  183.0 2.3 conditional.60
  195.7 11.6 %collective-permute-done.21 = bf16[1,8,128,128]{2,3,1,0:T(8,128)(2,1)S(1)} collective-permute-done((bf16[1,8,128,128]{2,3,1,0:T(8,128)(2,1)S(1)}, bf16[1,8,128,128]{2,3,1,0:T(8,128)(2,1)S(1)}, u32[]{:S(2)}, u32[]{:S(2)}) %collective-permute-start.21) | collective-permute-done | bytes 262176 | tf_op jit(solution)/shard_map/ppermute | solution.py:10
  207.9 8.7 %collective-permute-done.22 = bf16[1,8,128,128]{2,3,1,0:T(8,128)(2,1)S(1)} collective-permute-done((bf16[1,8,128,128]{2,3,1,0:T(8,128)(2,1)S(1)}, bf16[1,8,128,128]{2,3,1,0:T(8,128)(2,1)S(1)}, u32[]{:S(2)}, u32[]{:S(2)}) %collective-permute-start.22) | collective-permute-done | bytes 262176 | tf_op jit(solution)/shard_map/ppermute | solution.py:10
  216.9 15.2 %all_to_all.54 = bf16[1,8,384,128]{3,2,0,1:T(8,128)(2,1)S(1)} all-to-all(bf16[1,8,384,128]{3,2,0,1:T(8,128)(2,1)S(1)} %pad_maximum_fusion.1), channel_id=1, replica_groups=mesh['cannon'=128,'rep'=4] {'rep'}, dimensions={1} | all-to-all | bytes 1572864 | tf_op jit(solution)/shard_map/all_to_all | solution.py:16
  (219 shorter events, 91.5 us)
Async XLA Ops:
  2.0 13.1 %all-to-all-start = ((s32[4,1,2]{2,1,0:T(1,128)}), s32[4,1,2]{2,1,0:T(1,128)S(1)}, u32[]{:S(2)}, u32[]{:S(2)}) async-start(s32[4,1,2]{2,1,0:T(1,128)} %copy.162), calls=%async_computation | async-start | bytes 4096 | tf_op jit(solution)/shard_map/all_to_all | solution.py:108
  21.1 14.9 %all-to-all-start.1 = ((bf16[4,2,384,128]{3,2,1,0:T(8,128)(2,1)}), bf16[4,2,384,128]{3,2,1,0:T(8,128)(2,1)S(1)}, u32[]{:S(2)}, u32[]{:S(2)}) async-start(bf16[4,2,384,128]{3,2,1,0:T(8,128)(2,1)} %pad_maximum_fusion), calls=%async_computation.1 | async-start | bytes 1572864 | tf_op jit(solution)/shard_map/all_to_all | solution.py:16
  36.5 30.8 %collective-permute-start.4 = (bf16[1,8,128,128]{2,3,1,0:T(8,128)(2,1)S(1)}, bf16[1,8,128,128]{2,3,1,0:T(8,128)(2,1)S(1)}, u32[]{:S(2)}, u32[]{:S(2)}) collective-permute-start(bf16[1,8,128,128]{2,3,1,0:T(8,128)(2,1)S(1)} %get-tuple-element.1003), channel_id=1, source_target_pairs={{1,0},{2,1},{3,2},{4,3},{5,4},{6,5},{7,6},{8,7},{9,8},{10,9},{11,1... | collective-permute-start | bytes 786440 | tf_op jit(solution)/shard_map/ppermute | solution.py:10
  40.6 29.6 %collective-permute-start.5 = (bf16[1,8,128,128]{2,3,1,0:T(8,128)(2,1)S(1)}, bf16[1,8,128,128]{2,3,1,0:T(8,128)(2,1)S(1)}, u32[]{:S(2)}, u32[]{:S(2)}) collective-permute-start(bf16[1,8,128,128]{2,3,1,0:T(8,128)(2,1)S(1)} %get-tuple-element.1003), channel_id=1, source_target_pairs={{2,0},{3,1},{4,2},{5,3},{6,4},{7,5},{8,6},{9,7},{10,8},{11,9},{12,... | collective-permute-start | bytes 786440 | tf_op jit(solution)/shard_map/ppermute | solution.py:10
  49.9 22.8 %collective-permute-start.6 = (bf16[1,8,128,128]{2,3,1,0:T(8,128)(2,1)S(1)}, bf16[1,8,128,128]{2,3,1,0:T(8,128)(2,1)}, u32[]{:S(2)}, u32[]{:S(2)}) collective-permute-start(bf16[1,8,128,128]{2,3,1,0:T(8,128)(2,1)S(1)} %get-tuple-element.1003), channel_id=1, source_target_pairs={{3,0},{4,1},{5,2},{6,3},{7,4},{8,5},{9,6},{10,7},{11,8},{12,9},{13... | collective-permute-start | bytes 786440 | tf_op jit(solution)/shard_map/ppermute | solution.py:10
  60.0 24.0 %collective-permute-start.2 = (bf16[1,8,128,128]{2,3,1,0:T(8,128)(2,1)S(1)}, bf16[1,8,128,128]{2,3,1,0:T(8,128)(2,1)S(1)}, u32[]{:S(2)}, u32[]{:S(2)}) collective-permute-start(bf16[1,8,128,128]{2,3,1,0:T(8,128)(2,1)S(1)} %get-tuple-element.1003), channel_id=1, source_target_pairs={{510,0},{511,1},{0,2},{1,3},{2,4},{3,5},{4,6},{5,7},{6,8},{7,9},{8... | collective-permute-start | bytes 786440 | tf_op jit(solution)/shard_map/ppermute | solution.py:10
  62.2 24.6 %collective-permute-start.3 = (bf16[1,8,128,128]{2,3,1,0:T(8,128)(2,1)S(1)}, bf16[1,8,128,128]{2,3,1,0:T(8,128)(2,1)S(1)}, u32[]{:S(2)}, u32[]{:S(2)}) collective-permute-start(bf16[1,8,128,128]{2,3,1,0:T(8,128)(2,1)S(1)} %get-tuple-element.1003), channel_id=1, source_target_pairs={{511,0},{0,1},{1,2},{2,3},{3,4},{4,5},{5,6},{6,7},{7,8},{8,9},{9,1... | collective-permute-start | bytes 786440 | tf_op jit(solution)/shard_map/ppermute | solution.py:10
  67.3 23.0 %collective-permute-start = (bf16[1,8,128,128]{2,3,1,0:T(8,128)(2,1)S(1)}, bf16[1,8,128,128]{2,3,1,0:T(8,128)(2,1)}, u32[]{:S(2)}, u32[]{:S(2)}) collective-permute-start(bf16[1,8,128,128]{2,3,1,0:T(8,128)(2,1)S(1)} %get-tuple-element.1003), channel_id=1, source_target_pairs={{508,0},{509,1},{510,2},{511,3},{0,4},{1,5},{2,6},{3,7},{4,8},{5,9... | collective-permute-start | bytes 786440 | tf_op jit(solution)/shard_map/ppermute | solution.py:10
  70.2 28.4 %collective-permute-start.1 = (bf16[1,8,128,128]{2,3,1,0:T(8,128)(2,1)S(1)}, bf16[1,8,128,128]{2,3,1,0:T(8,128)(2,1)}, u32[]{:S(2)}, u32[]{:S(2)}) collective-permute-start(bf16[1,8,128,128]{2,3,1,0:T(8,128)(2,1)S(1)} %get-tuple-element.1003), channel_id=1, source_target_pairs={{509,0},{510,1},{511,2},{0,3},{1,4},{2,5},{3,6},{4,7},{5,8},{6,9},... | collective-permute-start | bytes 786440 | tf_op jit(solution)/shard_map/ppermute | solution.py:10
  72.7 50.2 %collective-permute-start.19 = (bf16[1,8,128,128]{2,3,1,0:T(8,128)(2,1)S(1)}, bf16[1,8,128,128]{2,3,1,0:T(8,128)(2,1)}, u32[]{:S(2)}, u32[]{:S(2)}) collective-permute-start(bf16[1,8,128,128]{2,3,1,0:T(8,128)(2,1)S(1)} %get-tuple-element.1004), channel_id=1, source_target_pairs={{2,0},{3,1},{4,2},{5,3},{6,4},{7,5},{8,6},{9,7},{10,8},{11,9},{12,... | collective-permute-start | bytes 786440 | tf_op jit(solution)/shard_map/ppermute | solution.py:10
  84.0 43.0 %collective-permute-start.20 = (bf16[1,8,128,128]{2,3,1,0:T(8,128)(2,1)S(1)}, bf16[1,8,128,128]{2,3,1,0:T(8,128)(2,1)}, u32[]{:S(2)}, u32[]{:S(2)}) collective-permute-start(bf16[1,8,128,128]{2,3,1,0:T(8,128)(2,1)S(1)} %get-tuple-element.1004), channel_id=1, source_target_pairs={{3,0},{4,1},{5,2},{6,3},{7,4},{8,5},{9,6},{10,7},{11,8},{12,9},{13... | collective-permute-start | bytes 786440 | tf_op jit(solution)/shard_map/ppermute | solution.py:10
  86.8 20.6 %collective-permute-start.18 = (bf16[1,8,128,128]{2,3,1,0:T(8,128)(2,1)S(1)}, bf16[1,8,128,128]{2,3,1,0:T(8,128)(2,1)S(1)}, u32[]{:S(2)}, u32[]{:S(2)}) collective-permute-start(bf16[1,8,128,128]{2,3,1,0:T(8,128)(2,1)S(1)} %get-tuple-element.1004), channel_id=1, source_target_pairs={{1,0},{2,1},{3,2},{4,3},{5,4},{6,5},{7,6},{8,7},{9,8},{10,9},{11,1... | collective-permute-start | bytes 786440 | tf_op jit(solution)/shard_map/ppermute | solution.py:10
  90.4 19.9 %collective-permute-start.16 = (bf16[1,8,128,128]{2,3,1,0:T(8,128)(2,1)S(1)}, bf16[1,8,128,128]{2,3,1,0:T(8,128)(2,1)}, u32[]{:S(2)}, u32[]{:S(2)}) collective-permute-start(bf16[1,8,128,128]{2,3,1,0:T(8,128)(2,1)S(1)} %get-tuple-element.1004), channel_id=1, source_target_pairs={{510,0},{511,1},{0,2},{1,3},{2,4},{3,5},{4,6},{5,7},{6,8},{7,9},{8... | collective-permute-start | bytes 786440 | tf_op jit(solution)/shard_map/ppermute | solution.py:10
  96.1 5.9 %copy-start.2 = (bf16[1,8,128,128]{3,2,0,1:T(8,128)(2,1)}, bf16[1,8,128,128]{3,2,0,1:T(8,128)(2,1)S(1)}, u32[]{:S(2)}) copy-start(bf16[1,8,128,128]{3,2,0,1:T(8,128)(2,1)S(1)} %add_dynamic-update-slice_fusion.7) | copy-start | bytes 786436
  98.6 15.2 %collective-permute-start.17 = (bf16[1,8,128,128]{2,3,1,0:T(8,128)(2,1)S(1)}, bf16[1,8,128,128]{2,3,1,0:T(8,128)(2,1)S(1)}, u32[]{:S(2)}, u32[]{:S(2)}) collective-permute-start(bf16[1,8,128,128]{2,3,1,0:T(8,128)(2,1)S(1)} %get-tuple-element.1004), channel_id=1, source_target_pairs={{511,0},{0,1},{1,2},{2,3},{3,4},{4,5},{5,6},{6,7},{7,8},{8,9},{9,1... | collective-permute-start | bytes 786440 | tf_op jit(solution)/shard_map/ppermute | solution.py:10
  107.4 23.5 %collective-permute-start.14 = (bf16[1,8,128,128]{2,3,1,0:T(8,128)(2,1)S(1)}, bf16[1,8,128,128]{2,3,1,0:T(8,128)(2,1)}, u32[]{:S(2)}, u32[]{:S(2)}) collective-permute-start(bf16[1,8,128,128]{2,3,1,0:T(8,128)(2,1)S(1)} %get-tuple-element.1004), channel_id=1, source_target_pairs={{508,0},{509,1},{510,2},{511,3},{0,4},{1,5},{2,6},{3,7},{4,8},{5,9... | collective-permute-start | bytes 786440 | tf_op jit(solution)/shard_map/ppermute | solution.py:10
  110.2 26.7 %collective-permute-start.15 = (bf16[1,8,128,128]{2,3,1,0:T(8,128)(2,1)S(1)}, bf16[1,8,128,128]{2,3,1,0:T(8,128)(2,1)}, u32[]{:S(2)}, u32[]{:S(2)}) collective-permute-start(bf16[1,8,128,128]{2,3,1,0:T(8,128)(2,1)S(1)} %get-tuple-element.1004), channel_id=1, source_target_pairs={{509,0},{510,1},{511,2},{0,3},{1,4},{2,5},{3,6},{4,7},{5,8},{6,9},... | collective-permute-start | bytes 786440 | tf_op jit(solution)/shard_map/ppermute | solution.py:10
  113.8 74.4 %collective-permute-start.26 = (bf16[1,8,128,128]{2,3,1,0:T(8,128)(2,1)S(1)}, bf16[1,8,128,128]{2,3,1,0:T(8,128)(2,1)}, u32[]{:S(2)}, u32[]{:S(2)}) collective-permute-start(bf16[1,8,128,128]{2,3,1,0:T(8,128)(2,1)S(1)} %get-tuple-element.1008), channel_id=1, source_target_pairs={{2,0},{3,1},{4,2},{5,3},{6,4},{7,5},{8,6},{9,7},{10,8},{11,9},{12,... | collective-permute-start | bytes 786440 | tf_op jit(solution)/shard_map/ppermute | solution.py:10
  122.9 4.0 %copy-start.6 = (bf16[1,8,128,128]{3,2,0,1:T(8,128)(2,1)}, bf16[1,8,128,128]{3,2,0,1:T(8,128)(2,1)S(1)}, u32[]{:S(2)}) copy-start(bf16[1,8,128,128]{3,2,0,1:T(8,128)(2,1)S(1)} %add_dynamic-update-slice_fusion.3) | copy-start | bytes 786436
  123.0 27.1 %collective-permute-start.12 = (bf16[1,8,128,128]{3,2,0,1:T(8,128)(2,1)S(1)}, bf16[1,8,128,128]{3,2,0,1:T(8,128)(2,1)S(1)}, u32[]{:S(2)}, u32[]{:S(2)}) collective-permute-start(bf16[1,8,128,128]{3,2,0,1:T(8,128)(2,1)S(1)} %subtract_convert_fusion), channel_id=1, source_target_pairs={{2,0},{3,1},{4,2},{5,3},{6,4},{7,5},{8,6},{9,7},{10,8},{11,9},{12,... | collective-permute-start | bytes 786440 | tf_op jit(solution)/shard_map/ppermute | solution.py:10
  127.0 20.2 %collective-permute-start.11 = (bf16[1,8,128,128]{3,2,0,1:T(8,128)(2,1)S(1)}, bf16[1,8,128,128]{3,2,0,1:T(8,128)(2,1)}, u32[]{:S(2)}, u32[]{:S(2)}) collective-permute-start(bf16[1,8,128,128]{3,2,0,1:T(8,128)(2,1)S(1)} %subtract_convert_fusion), channel_id=1, source_target_pairs={{1,0},{2,1},{3,2},{4,3},{5,4},{6,5},{7,6},{8,7},{9,8},{10,9},{11,1... | collective-permute-start | bytes 786440 | tf_op jit(solution)/shard_map/ppermute | solution.py:10
  130.9 21.9 %collective-permute-start.13 = (bf16[1,8,128,128]{3,2,0,1:T(8,128)(2,1)S(1)}, bf16[1,8,128,128]{3,2,0,1:T(8,128)(2,1)S(1)}, u32[]{:S(2)}, u32[]{:S(2)}) collective-permute-start(bf16[1,8,128,128]{3,2,0,1:T(8,128)(2,1)S(1)} %subtract_convert_fusion), channel_id=1, source_target_pairs={{3,0},{4,1},{5,2},{6,3},{7,4},{8,5},{9,6},{10,7},{11,8},{12,9},{13... | collective-permute-start | bytes 786440 | tf_op jit(solution)/shard_map/ppermute | solution.py:10
  136.9 19.9 %collective-permute-start.9 = (bf16[1,8,128,128]{3,2,0,1:T(8,128)(2,1)S(1)}, bf16[1,8,128,128]{3,2,0,1:T(8,128)(2,1)S(1)}, u32[]{:S(2)}, u32[]{:S(2)}) collective-permute-start(bf16[1,8,128,128]{3,2,0,1:T(8,128)(2,1)S(1)} %subtract_convert_fusion), channel_id=1, source_target_pairs={{510,0},{511,1},{0,2},{1,3},{2,4},{3,5},{4,6},{5,7},{6,8},{7,9},{8... | collective-permute-start | bytes 786440 | tf_op jit(solution)/shard_map/ppermute | solution.py:10
  147.2 20.0 %collective-permute-start.10 = (bf16[1,8,128,128]{3,2,0,1:T(8,128)(2,1)S(1)}, bf16[1,8,128,128]{3,2,0,1:T(8,128)(2,1)}, u32[]{:S(2)}, u32[]{:S(2)}) collective-permute-start(bf16[1,8,128,128]{3,2,0,1:T(8,128)(2,1)S(1)} %subtract_convert_fusion), channel_id=1, source_target_pairs={{511,0},{0,1},{1,2},{2,3},{3,4},{4,5},{5,6},{6,7},{7,8},{8,9},{9,1... | collective-permute-start | bytes 786440 | tf_op jit(solution)/shard_map/ppermute | solution.py:10
  150.0 21.3 %collective-permute-start.7 = (bf16[1,8,128,128]{3,2,0,1:T(8,128)(2,1)S(1)}, bf16[1,8,128,128]{3,2,0,1:T(8,128)(2,1)}, u32[]{:S(2)}, u32[]{:S(2)}) collective-permute-start(bf16[1,8,128,128]{3,2,0,1:T(8,128)(2,1)S(1)} %subtract_convert_fusion), channel_id=1, source_target_pairs={{508,0},{509,1},{510,2},{511,3},{0,4},{1,5},{2,6},{3,7},{4,8},{5,9... | collective-permute-start | bytes 786440 | tf_op jit(solution)/shard_map/ppermute | solution.py:10
  152.8 25.9 %collective-permute-start.8 = (bf16[1,8,128,128]{3,2,0,1:T(8,128)(2,1)S(1)}, bf16[1,8,128,128]{3,2,0,1:T(8,128)(2,1)}, u32[]{:S(2)}, u32[]{:S(2)}) collective-permute-start(bf16[1,8,128,128]{3,2,0,1:T(8,128)(2,1)S(1)} %subtract_convert_fusion), channel_id=1, source_target_pairs={{509,0},{510,1},{511,2},{0,3},{1,4},{2,5},{3,6},{4,7},{5,8},{6,9},... | collective-permute-start | bytes 786440 | tf_op jit(solution)/shard_map/ppermute | solution.py:10
  156.8 34.7 %collective-permute-start.27 = (bf16[1,8,128,128]{2,3,1,0:T(8,128)(2,1)S(1)}, bf16[1,8,128,128]{2,3,1,0:T(8,128)(2,1)}, u32[]{:S(2)}, u32[]{:S(2)}) collective-permute-start(bf16[1,8,128,128]{2,3,1,0:T(8,128)(2,1)S(1)} %get-tuple-element.1008), channel_id=1, source_target_pairs={{3,0},{4,1},{5,2},{6,3},{7,4},{8,5},{9,6},{10,7},{11,8},{12,9},{13... | collective-permute-start | bytes 786440 | tf_op jit(solution)/shard_map/ppermute | solution.py:10
  167.2 18.1 %collective-permute-start.25 = (bf16[1,8,128,128]{2,3,1,0:T(8,128)(2,1)S(1)}, bf16[1,8,128,128]{2,3,1,0:T(8,128)(2,1)}, u32[]{:S(2)}, u32[]{:S(2)}) collective-permute-start(bf16[1,8,128,128]{2,3,1,0:T(8,128)(2,1)S(1)} %get-tuple-element.1008), channel_id=1, source_target_pairs={{1,0},{2,1},{3,2},{4,3},{5,4},{6,5},{7,6},{8,7},{9,8},{10,9},{11,1... | collective-permute-start | bytes 786440 | tf_op jit(solution)/shard_map/ppermute | solution.py:10
  171.4 22.5 %collective-permute-start.23 = (bf16[1,8,128,128]{2,3,1,0:T(8,128)(2,1)S(1)}, bf16[1,8,128,128]{2,3,1,0:T(8,128)(2,1)}, u32[]{:S(2)}, u32[]{:S(2)}) collective-permute-start(bf16[1,8,128,128]{2,3,1,0:T(8,128)(2,1)S(1)} %get-tuple-element.1008), channel_id=1, source_target_pairs={{510,0},{511,1},{0,2},{1,3},{2,4},{3,5},{4,6},{5,7},{6,8},{7,9},{8... | collective-permute-start | bytes 786440 | tf_op jit(solution)/shard_map/ppermute | solution.py:10
  178.7 16.9 %collective-permute-start.24 = (bf16[1,8,128,128]{2,3,1,0:T(8,128)(2,1)S(1)}, bf16[1,8,128,128]{2,3,1,0:T(8,128)(2,1)}, u32[]{:S(2)}, u32[]{:S(2)}) collective-permute-start(bf16[1,8,128,128]{2,3,1,0:T(8,128)(2,1)S(1)} %get-tuple-element.1008), channel_id=1, source_target_pairs={{511,0},{0,1},{1,2},{2,3},{3,4},{4,5},{5,6},{6,7},{7,8},{8,9},{9,1... | collective-permute-start | bytes 786440 | tf_op jit(solution)/shard_map/ppermute | solution.py:10
  185.4 22.0 %collective-permute-start.21 = (bf16[1,8,128,128]{2,3,1,0:T(8,128)(2,1)S(1)}, bf16[1,8,128,128]{2,3,1,0:T(8,128)(2,1)S(1)}, u32[]{:S(2)}, u32[]{:S(2)}) collective-permute-start(bf16[1,8,128,128]{2,3,1,0:T(8,128)(2,1)S(1)} %get-tuple-element.1008), channel_id=1, source_target_pairs={{508,0},{509,1},{510,2},{511,3},{0,4},{1,5},{2,6},{3,7},{4,8},{5,9... | collective-permute-start | bytes 786440 | tf_op jit(solution)/shard_map/ppermute | solution.py:10
  188.2 28.4 %collective-permute-start.22 = (bf16[1,8,128,128]{2,3,1,0:T(8,128)(2,1)S(1)}, bf16[1,8,128,128]{2,3,1,0:T(8,128)(2,1)S(1)}, u32[]{:S(2)}, u32[]{:S(2)}) collective-permute-start(bf16[1,8,128,128]{2,3,1,0:T(8,128)(2,1)S(1)} %get-tuple-element.1008), channel_id=1, source_target_pairs={{509,0},{510,1},{511,2},{0,3},{1,4},{2,5},{3,6},{4,7},{5,8},{6,9},... | collective-permute-start | bytes 786440 | tf_op jit(solution)/shard_map/ppermute | solution.py:10
  (6 other events, 13.6 us)
where the time goes:
time: 235 us; the launch traced here: 233 us
  starting transfers between devices  113 us (48%)
  waiting for transfers between devices  39.2 us (17%)
  local copies, waits for them, and re-layouts  24 us (10%)
  blocking collectives  21.3 us (9%)
  other arithmetic  15.3 us (7%)
  matrix products  12.3 us (5%)
  between operations  6.59 us (3%)
    ppermute x28, starting transfers between devices, from_behind(): return lax.ppermute(block, axis, route)  99 us
    ppermute x28, waiting for transfers between devices, from_behind(): return lax.ppermute(block, axis, route)  28.4 us
    all_to_all x1, blocking collectives, side_by_side(): lax.all_to_all(both, axis, split_axis=split_dim, concat_axis=concat_dim,...  15.2 us
    dot_general x20, matrix products, compute_slot(): jnp.einsum('ipq,itqr->itpr', factor_block, window, preferred_element_type...  12.3 us
    all_to_all x1, waiting for transfers between devices, side_by_side(): lax.all_to_all(both, axis, split_axis=split_dim, concat_axis=concat_dim,...  10.6 us
    all_to_all x1, starting transfers between devices, body(): lax.all_to_all(margin_mask, 'rep', split_axis=0, concat_axis=1, tiled=True)  10.1 us
    another operation x38, local copies, waits for them, and re-layouts  8.2 us
    cond x20, local copies, waits for them, and re-layouts, row_product(): lax.cond(present, compute_slot, skip_slot)  6.87 us
  transfers between devices with their start and end apart: 30, of which 7 were waited for; matrix products, arithmetic and copies ran while one was open for 20% of the time, Pallas kernels for 0%

commit v1 on v0

v1 whole, which is shorter than its diff:
```python
import jax
import jax.numpy as jnp
from jax import lax
from jax.experimental import pallas as pl
from jax.experimental.pallas import tpu as pltpu
from jax.sharding import PartitionSpec as P

MESH = pl.DeviceIdType.MESH
BLK = 128
NS = 8
HALF = 4
ROWS = 4
Z_PANELS = 32
SPAN = ROWS + NS - 1


def rect(j, slots):
    return (j + HALF, j + min(slots), len(slots)) if slots else None


def slots_of(role):
    return (2 * role, 2 * role + 1)


def pick(role, allowed):
    return [u for u in slots_of(role) if u in allowed]


def need_up(j):
    return range(HALF - j, NS)


def need_down(j):
    return range(0, NS - 1 - j) if j < 3 else ()


def shift(area, link):
    move = {"p": -ROWS, "P": -ROWS, "m": ROWS, "M": ROWS}.get(link, 0)
    return (area[0] + move, area[1] + move, area[2])


EVERY = (0, 1, 2, 3)
FLIP = {"c": 1, "z": 2, "p": 0, "m": 0, "P": 2, "M": 2}
PLAIN, LAST, FIRST = 0, 1, 2
KINDS = (PLAIN, LAST, FIRST)
ENDS = {
    (None, False): (KINDS, KINDS),
    ("p", False): ((PLAIN, FIRST), (PLAIN, LAST)),
    ("p", True): ((LAST,), (FIRST,)),
    ("m", False): ((PLAIN, LAST), (PLAIN, FIRST)),
    ("m", True): ((FIRST,), (LAST,)),
}


class Message:
    def __init__(self, array, link, areas, index, senders, receivers):
        self.array, self.link, self.areas, self.index = array, link, areas, index
        self.senders, self.receivers = senders, receivers


class Table:
    def __init__(self):
        self.rows = {}

    def put(self, name, array, link, areas, senders, receivers):
        areas = {role: area for role, area in areas.items() if area is not None}
        if areas:
            self.rows[name] = Message(array, link, areas, len(self.rows), senders, receivers)

    def add(self, name, link, areas, far=False):
        way = link.lower() if link in "pPmM" else None
        self.put(name, name[0], link, areas, *ENDS[way, far])

    def relay(self, name, link, of, roles=EVERY, keep=None):
        row = self.rows.get(of)
        if row is None:
            return
        got = {}
        for role in roles:
            sender = role ^ FLIP[row.link]
            if sender in row.areas:
                area = shift(row.areas[sender], row.link)
                got[role] = area if keep is None else keep(area)
        senders = row.receivers
        receivers = senders
        if link in "pm":
            ends = ENDS[link, False]
            senders, receivers = tuple(k for k in ends[0] if k in senders), ends[1]
        self.put(name, name[0], link, got, senders, receivers)


def within(area, row, low, high):
    first, end = max(area[1], low), min(area[1] + area[2], high)
    return (area[0], first, end - first) if end > first else None


def build_table():
    t = Table()
    for j in range(ROWS):
        low, high = range(HALF - j, HALF), range(HALF, NS - 1 - j)
        up, down = need_up(j), need_down(j)
        own = {r: rect(j, slots_of(r)) for r in EVERY}

        def some(allowed, roles=EVERY, other=0):
            return {r: rect(j, pick(r ^ other, allowed)) for r in roles}

        for a in "RI":
            t.add((a, "zo", j), "z", own)
            t.add((a, "co", j), "c", own)
            t.relay((a, "cz", j), "c", (a, "zo", j))
            t.add((a, "po", j), "p", some(up))
            t.add((a, "mo", j), "m", some(down))
            t.add((a, "mz", j), "m", some(down, EVERY, 2))
            t.relay((a, "cpo", j), "c", (a, "po", j))
            t.relay((a, "cmo", j), "c", (a, "mo", j))
            t.relay((a, "cmz", j), "c", (a, "mz", j))
        t.add(("R", "pz", j), "p", some(up, EVERY, 2))
        t.relay(("R", "cpz", j), "c", ("R", "pz", j))
        t.relay(("I", "zpo", j), "z", ("I", "po", j))
        t.relay(("I", "czpo", j), "c", ("I", "zpo", j))
        for a, plus, minus in (("R", "P", "M"), ("I", "p", "m")):
            t.add((a, "Xpo", j), plus, some(up, (2, 3)), True)
            t.add((a, "Xpz", j), plus, some(up, (2, 3), 2), True)
            t.add((a, "Xmo", j), minus, some(down, (0, 1)), True)
            t.add((a, "Xmz", j), minus, some(down, (0, 1), 2), True)
            for end in ("po", "pz", "mo", "mz"):
                t.relay((a, "Xc" + end, j), "c", (a, "X" + end, j))
                t.relay((a, "Xz" + end, j), "z", (a, "X" + end, j))
                t.relay((a, "Xcz" + end, j), "c", (a, "Xz" + end, j))

        t.add(("H", "co", j), "c", own)
        t.add(("H", "zo", j), "z", {r: rect(j, pick(r, low if r < 2 else high)) for r in EVERY})
        t.relay(("H", "cz", j), "c", ("H", "zo", j))
        t.relay(("H", "pz", j), "p", ("H", "zo", j), (0, 1))
        t.relay(("H", "cpz", j), "c", ("H", "pz", j))
        beyond = range(NS - 1 - j, NS)
        t.add(("H", "po", j), "p", {r: rect(j, pick(r, low if r < 2 else beyond)) for r in EVERY})
        t.relay(("H", "cpo", j), "c", ("H", "po", j))
        t.relay(("H", "zpo", j), "z", ("H", "po", j), (2, 3))
        t.relay(("H", "czpo", j), "c", ("H", "zpo", j))
        t.add(("H", "Xpo", j), "P", some(up, (2, 3)), True)
        t.add(("H", "Xpz", j), "P", some(low, (2, 3), 2), True)
        t.relay(("H", "Xcpo", j), "c", ("H", "Xpo", j))
        t.relay(("H", "Xcpz", j), "c", ("H", "Xpz", j))
        t.relay(("H", "Xzpo", j), "z", ("H", "Xpo", j), EVERY, lambda area: within(area, j, HALF, SPAN))
        t.relay(("H", "Xczpo", j), "c", ("H", "Xzpo", j))
        if j < 3:
            t.add(("H", "mo", j), "m", {r: rect(j, pick(r, range(HALF) if r < 2 else high)) for r in EVERY})
            t.relay(("H", "cmo", j), "c", ("H", "mo", j))
            t.relay(("H", "zmo", j), "z", ("H", "mo", j), (0, 1), lambda area: within(area, j, area[0] - HALF + 1, SPAN))
            t.relay(("H", "czmo", j), "c", ("H", "zmo", j))
            t.add(("H", "Xmo", j), "M", some(range(1, HALF), (0, 1)), True)
            t.add(("H", "Xmz", j), "M", some(high, (0, 1), 2), True)
            t.add(("H", "Xml", j), "m", some(range(0, 3 - j), (0, 1)), True)
            for end in ("mo", "mz", "ml"):
                t.relay(("H", "Xc" + end, j), "c", ("H", "X" + end, j))

        core = 0 if j in (0, 3) else 1
        wide, few = rect(j, up), rect(j, range(NS - j, NS))
        t.add(("P", "p", j), "p", {core: wide, 2 + core: few})
        t.relay(("P", "cp", j), "c", ("P", "p", j))
        t.add(("P", "Xp", j), "P", {2 + core: wide}, True)
        t.add(("P", "Xq", j), "p", {2 + core: few}, True)
        if j < 3:
            few, wide = rect(j, range(0, 3 - j)), rect(j, range(1, NS - 1 - j))
            t.add(("P", "m", j), "m", {core: few, 2 + core: wide})
            t.relay(("P", "cm", j), "c", ("P", "m", j))
            t.add(("P", "Xm", j), "M", {core: wide}, True)
            t.add(("P", "Xn", j), "m", {core: few}, True)
        for end in ("p", "q", "m", "n"):
            t.relay(("P", "Xc" + end, j), "c", ("P", "X" + end, j))
    for name, link in (("zo", "z"), ("co", "c"), ("cz", "c")):
        t.add(("M", name, 0), link, {r: (r ^ 2 if name == "cz" else r, 0, 1) for r in EVERY})
    return t


TABLE = build_table()


def view(refs, array, area):
    row, col, wide = area
    if array == "M":
        return refs["M"].at[pl.ds(row * 8, 8), :]
    return refs[array].at[pl.ds(row * BLK, BLK), pl.ds(col * BLK, wide * BLK)]


class Role:
    def __init__(self, kind, role, refs, send_sem, recv_sem, cannon, panels):
        self.kind, self.role, self.refs = kind, role, refs
        self.send_sem, self.recv_sem = send_sem, recv_sem
        self.cannon, self.panels = cannon, panels

    def copy(self, row, sender):
        area = row.areas[sender]
        panel = self.cannon
        if row.link in "pP":
            panel = lax.rem(self.cannon + 1, self.panels)
        if row.link in "mM":
            panel = lax.rem(self.cannon + self.panels - 1, self.panels)
        return pltpu.make_async_remote_copy(
            src_ref=view(self.refs, row.array, area),
            dst_ref=view(self.refs, row.array, shift(area, row.link)),
            send_sem=self.send_sem.at[row.index],
            recv_sem=self.recv_sem.at[row.index],
            device_id=(panel, self.role ^ FLIP[row.link]),
            device_id_type=MESH,
        )

    def send_one(self, name):
        row = TABLE.rows.get(name)
        if row is not None and self.kind in row.senders and self.role in row.areas:
            self.copy(row, self.role).start()

    def recv_one(self, name):
        row = TABLE.rows.get(name)
        if row is None or self.kind not in row.receivers:
            return False
        sender = self.role ^ FLIP[row.link]
        if sender not in row.areas:
            return False
        self.copy(row, sender).wait_recv()
        return True

    def send(self, array, *ends):
        for j in range(ROWS):
            for end in ends:
                self.send_one((array, end, j))

    def recv(self, array, *ends):
        for j in range(ROWS):
            for end in ends:
                self.recv_one((array, end, j))

    def pass_on(self, array, end, *onward):
        for j in range(ROWS):
            if self.recv_one((array, end, j)):
                for then in onward:
                    self.send_one((array, then, j))

    def drain(self):
        for row in TABLE.rows.values():
            if self.kind in row.senders and self.role in row.areas:
                self.copy(row, self.role).wait_send()


def kernel(panels, root_in, inverse_in, hamilton_in, margin_in, hamilton_mask_in,
           root_out, inverse_out, lowdin_out,
           root, inverse, hamilton, poly, margin, next_rows, send_sem, recv_sem):
    cannon, rep = lax.axis_index("cannon"), lax.axis_index("rep")
    refs = {"R": root, "I": inverse, "H": hamilton, "P": poly, "M": margin}
    ahead, behind = lax.rem(cannon + 1, panels), lax.rem(cannon + panels - 1, panels)
    sibling, across = rep + 1 - 2 * lax.rem(rep, 2), lax.rem(rep + 2, 4)

    place = lax.rem(cannon, Z_PANELS)
    far = ((place == Z_PANELS - 1) & (rep >= 2)) | ((place == 0) & (rep < 2))
    beyond = lax.rem(cannon + jnp.where(place == 0, panels - 1, 1), panels)

    barrier = pltpu.get_barrier_semaphore()
    for peer in ((ahead, rep), (behind, rep), (cannon, sibling), (cannon, across)):
        pl.semaphore_signal(barrier, inc=1, device_id=peer, device_id_type=MESH)

    @pl.when(far)
    def _():
        pl.semaphore_signal(barrier, inc=1, device_id=(beyond, across), device_id_type=MESH)

    for array, source, scale in (
        (root, root_in, margin_in), (inverse, inverse_in, margin_in), (hamilton, hamilton_in, hamilton_mask_in),
    ):
        for j in range(ROWS):
            for b in range(2):
                keep = scale[b, j].astype(jnp.float32).astype(jnp.bfloat16)
                at = pl.multiple_of((j + 2 * rep + b) * BLK, BLK)
                array[pl.ds((j + HALF) * BLK, BLK), pl.ds(at, BLK)] = source[j, b] * keep
    for j in range(ROWS):
        for b in range(2):
            keep = margin_in[b, j].astype(jnp.float32)
            margin[pl.ds(rep * 8 + j * 2 + b, 1), :] = jnp.full((1, BLK), keep, jnp.float32)
    for array in (root, inverse, hamilton, poly):
        for row in range(SPAN):
            right = row + HALF
            if right < SPAN:
                array[row * BLK:(row + 1) * BLK, right * BLK:] = jnp.zeros((BLK, (SPAN - right) * BLK), jnp.bfloat16)
            left = row - HALF
            if left > 0:
                array[row * BLK:(row + 1) * BLK, :left * BLK] = jnp.zeros((BLK, left * BLK), jnp.bfloat16)

    @pl.when(far)
    def _():
        pl.semaphore_wait(barrier, 5)

    @pl.when(jnp.logical_not(far))
    def _():
        pl.semaphore_wait(barrier, 4)

    def by_role(plan):
        for kind in KINDS:
            here = {PLAIN: (place > 0) & (place < Z_PANELS - 1), LAST: place == Z_PANELS - 1, FIRST: place == 0}[kind]
            for role in EVERY:
                @pl.when(here & (rep == role))
                def _():
                    plan(Role(kind, role, refs, send_sem, recv_sem, cannon, panels))

    def gather(d):
        d.send("R", "zo", "co")
        d.send("R", "po", "mo", "Xpo", "Xmo")
        d.send("M", "zo", "co")
        d.send("I", "zo", "co")
        d.pass_on("R", "zo", "cz", "pz", "mz", "Xpz", "Xmz")
        d.send("I", "po", "mo", "Xpo", "Xmo")
        d.pass_on("M", "zo", "cz")
        d.pass_on("R", "po", "cpo")
        d.pass_on("R", "mo", "cmo")
        d.send("H", "zo", "co", "po", "mo", "Xpo", "Xmo", "Xml")
        d.pass_on("I", "zo", "cz", "mz", "Xmz", "Xpz")
        d.pass_on("R", "pz", "cpz")
        d.pass_on("R", "mz", "cmz")
        for end in ("po", "mo", "pz", "mz"):
            d.pass_on("R", "X" + end, "Xz" + end, "Xc" + end)
        d.pass_on("I", "po", "cpo", "zpo")
        d.pass_on("H", "zo", "cz", "pz", "Xpz", "Xmz")
        for end in ("po", "mo", "pz", "mz"):
            d.pass_on("R", "Xz" + end, "Xcz" + end)
        d.recv("M", "co", "cz")
        d.recv("I", "co", "cz")
        d.recv("R", "co", "cz", "cpo", "cpz", "cmo", "cmz")
        for end in ("po", "mo", "pz", "mz"):
            d.recv("R", "Xc" + end, "Xcz" + end)

    by_role(gather)

    def mask_row(i):
        return jnp.concatenate([margin[(t // 2) * 8 + i * 2 + t % 2:(t // 2) * 8 + i * 2 + t % 2 + 1, :]
                                for t in range(NS)], axis=1)

    def window(i):
        return slice(i * BLK, (i + NS) * BLK)

    def own(i):
        return slice((i + HALF) * BLK, (i + HALF + 1) * BLK)

    at_row = lax.broadcasted_iota(jnp.int32, (BLK, NS * BLK), 0)
    at_col = lax.broadcasted_iota(jnp.int32, (BLK, NS * BLK), 1)
    diagonal = jnp.where(at_col - HALF * BLK == at_row, 1.5, 0.0).astype(jnp.float32)
    for i in range(ROWS):
        product = jnp.dot(inverse[own(i), window(i)], root[window(i), window(i)], preferred_element_type=jnp.float32)
        poly[own(i), window(i)] = (diagonal - 0.5 * (product * mask_row(i))).astype(jnp.bfloat16)

    def exchange(d):
        d.send("P", "p", "m", "Xp", "Xq", "Xm", "Xn")
        d.pass_on("I", "mo", "cmo")
        d.pass_on("I", "mz", "cmz")
        for end in ("po", "mo", "pz", "mz"):
            d.pass_on("I", "X" + end, "Xz" + end, "Xc" + end)
        d.pass_on("I", "zpo", "czpo")
        d.pass_on("H", "po", "cpo", "zpo")
        d.pass_on("H", "mo", "cmo", "zmo")
        d.pass_on("H", "pz", "cpz")
        for end in ("po", "mo", "pz", "mz"):
            d.pass_on("I", "Xz" + end, "Xcz" + end)
        d.recv("I", "cpo", "cmo", "cmz", "czpo")
        for end in ("po", "mo", "pz", "mz"):
            d.recv("I", "Xc" + end, "Xcz" + end)

    by_role(exchange)

    for i in range(ROWS):
        product = jnp.dot(poly[own(i), window(i)], inverse[window(i), window(i)], preferred_element_type=jnp.float32)
        next_rows[i] = (product * mask_row(i)).astype(jnp.bfloat16)
        mine = next_rows[i, :, pl.ds(pl.multiple_of(2 * rep * BLK, 2 * BLK), 2 * BLK)]
        for b in range(2):
            inverse_out[i, b] = mine[:, b * BLK:(b + 1) * BLK]

    def settle(d):
        d.pass_on("H", "zpo", "czpo")
        d.pass_on("H", "zmo", "czmo")
        d.pass_on("H", "Xpo", "Xzpo", "Xcpo")
        d.pass_on("H", "Xpz", "Xcpz")
        for end in ("mo", "mz", "ml"):
            d.pass_on("H", "X" + end, "Xc" + end)
        d.pass_on("H", "Xzpo", "Xczpo")
        d.pass_on("P", "p", "cp")
        d.pass_on("P", "m", "cm")
        for end in ("q", "n", "p", "m"):
            d.pass_on("P", "X" + end, "Xc" + end)
        d.recv("H", "co", "cz", "cpo", "cpz", "cmo", "czpo", "czmo")
        d.recv("H", "Xcpo", "Xcpz", "Xczpo", "Xcmo", "Xcmz", "Xcml")

    by_role(settle)

    def narrow(first, second, i):
        cols = pl.ds(pl.multiple_of((i + 2 * rep) * BLK, BLK), 2 * BLK)
        return jnp.dot(first, second[window(i), cols], preferred_element_type=jnp.float32)

    for i in range(ROWS):
        product = narrow(next_rows[i], hamilton, i)
        for b in range(2):
            keep = hamilton_mask_in[b, i].astype(jnp.float32)
            lowdin_out[i, b] = (product[:, b * BLK:(b + 1) * BLK] * keep).astype(jnp.bfloat16)

    def last(d):
        d.recv("P", "cp", "cm", "Xcp", "Xcq", "Xcm", "Xcn")

    by_role(last)

    for i in range(ROWS):
        product = narrow(root[own(i), window(i)], poly, i)
        for b in range(2):
            keep = margin_in[b, i].astype(jnp.float32)
            root_out[i, b] = (product[:, b * BLK:(b + 1) * BLK] * keep).astype(jnp.bfloat16)

    def finish(d):
        d.drain()

    by_role(finish)


def solution(mesh):
    panels = mesh.shape["cannon"]
    count = len(TABLE.rows)
    vmem = pl.BlockSpec(memory_space=pltpu.VMEM)
    smem = pl.BlockSpec(memory_space=pltpu.SMEM)

    def body(root_margin, inverse_root, hamiltonian, margin_mask, hamilton_mask):
        shape = jax.ShapeDtypeStruct(root_margin.shape, jnp.bfloat16)

        def run(*refs):
            kernel(panels, *refs)

        band = pltpu.VMEM((SPAN * BLK, SPAN * BLK), jnp.bfloat16)
        return pl.pallas_call(
            run,
            out_shape=(shape, shape, shape),
            in_specs=[vmem, vmem, vmem, smem, smem],
            out_specs=(vmem, vmem, vmem),
            scratch_shapes=[
                band, band, band, band,
                pltpu.VMEM((4 * 8, BLK), jnp.float32),
                pltpu.VMEM((ROWS, BLK, NS * BLK), jnp.bfloat16),
                pltpu.SemaphoreType.DMA((count,)),
                pltpu.SemaphoreType.DMA((count,)),
            ],
            compiler_params=pltpu.CompilerParams(
                collective_id=0, has_side_effects=True, vmem_limit_bytes=48 << 20
            ),
            cost_estimate=pl.CostEstimate(flops=4 * 4 * 268435456, bytes_accessed=6 * 262144, transcendentals=0),
            name="newton_step",
        )(root_margin, inverse_root, hamiltonian, margin_mask.T, hamilton_mask.T)

    spec = P("cannon", "rep", None, None)
    mask = P("cannon", "rep")
    return jax.shard_map(body, mesh=mesh, in_specs=(spec, spec, spec, mask, mask),
                         out_specs=(spec, spec, spec), check_vma=False)
```

time: 235 us -> 69.8 us (0.30)
  starting transfers between devices: 113 us -> 0 us
  Pallas kernels: 0 us -> 62.8 us
  waiting for transfers between devices: 39.2 us -> 0 us
  blocking collectives: 21.3 us -> 0 us
  local copies, waits for them, and re-layouts: 24 us -> 5.64 us
  other arithmetic: 15.3 us -> 0 us
  matrix products: 12.3 us -> 0 us
  between operations: 6.59 us -> 0.66 us
    ppermute x28 -> x0, starting transfers between devices: 99 us -> none  [from_behind(): return lax.ppermute(block, axis, route)]
    pallas_call x0 -> x1, Pallas kernels: none -> 62.8 us  [body(): pl.pallas_call(run, out_shape=(shape, shape, shape), in_specs=[vmem, vmem...]
    ppermute x28 -> x0, waiting for transfers between devices: 28.4 us -> none  [from_behind(): return lax.ppermute(block, axis, route)]
    all_to_all x2 -> x0, blocking collectives: 21.3 us -> none  [the longest x1 15.2 us: side_by_side(): lax.all_to_all(both, axis, split_axis=split_dim, concat_axis=concat_dim,...]
    all_to_all x2 -> x0, starting transfers between devices: 14.2 us -> none  [the longest x1 10.1 us: body(): lax.all_to_all(margin_mask, 'rep', split_axis=0, concat_axis=1, tiled=True)]
    dot_general x20 -> x0, matrix products: 12.3 us -> none  [compute_slot(): jnp.einsum('ipq,itqr->itpr', factor_block, window, preferred_element_type...]
    all_to_all x2 -> x0, waiting for transfers between devices: 10.7 us -> none  [the longest x1 10.6 us: side_by_side(): lax.all_to_all(both, axis, split_axis=split_dim, concat_axis=concat_dim,...]
    another operation x38 -> x0, local copies, waits for them, and re-layouts: 8.2 us -> none
  transfers between devices with their start and end apart: 30 -> 0, of which waited for: 7 -> 0; matrix products, arithmetic and copies ran while one was open for 20% -> 0% of each run, Pallas kernels for 0% -> 0%
where the time goes in v1:
time: 69.8 us; the launch traced here: 69.1 us
  Pallas kernels  62.8 us (90%)
  local copies, waits for them, and re-layouts  5.64 us (8%)
    pallas_call x1, Pallas kernels, body(): pl.pallas_call(run, out_shape=(shape, shape, shape), in_specs=[vmem, vmem...  62.8 us
    unnamed x13, local copies, waits for them, and re-layouts  5.64 us

profile of v1, /device:TPU:1, one launch (start us, length us, event | category | flops | bytes accessed | tf_op | source)
XLA Modules:
  0.0 69.1 jit_solution(2567179922748398874)
XLA Ops:
  0.6 0.0 copy-start.4
  0.6 0.0 copy-start.3
  0.7 0.7 copy-done.4
  1.3 0.0 copy-done.3
  1.3 0.0 copy-start
  1.3 0.9 %copy-done = bf16[4,2,128,128]{3,2,1,0:T(8,128)(2,1)S(1)} copy-done((bf16[4,2,128,128]{3,2,1,0:T(8,128)(2,1)S(1)}, bf16[4,2,128,128]{3,2,1,0:T(8,128)(2,1)}, u32[]{:S(2)}) %copy-start) | copy-done | bytes 262168
  2.3 0.0 copy-start.1
  2.3 0.9 %copy-done.1 = bf16[4,2,128,128]{3,2,1,0:T(8,128)(2,1)S(1)} copy-done((bf16[4,2,128,128]{3,2,1,0:T(8,128)(2,1)S(1)}, bf16[4,2,128,128]{3,2,1,0:T(8,128)(2,1)}, u32[]{:S(2)}) %copy-start.1) | copy-done | bytes 262168
  3.2 0.0 copy-start.2
  3.2 0.9 %copy-done.2 = bf16[4,2,128,128]{3,2,1,0:T(8,128)(2,1)S(1)} copy-done((bf16[4,2,128,128]{3,2,1,0:T(8,128)(2,1)S(1)}, bf16[4,2,128,128]{3,2,1,0:T(8,128)(2,1)}, u32[]{:S(2)}) %copy-start.2) | copy-done | bytes 262168
  4.2 62.8 %newton_step.1 = (bf16[4,2,128,128]{3,2,1,0:T(8,128)(2,1)S(1)}, bf16[4,2,128,128]{3,2,1,0:T(8,128)(2,1)S(1)}, bf16[4,2,128,128]{3,2,1,0:T(8,128)(2,1)S(1)}) custom-call(bf16[4,2,128,128]{3,2,1,0:T(8,128)(2,1)S(1)} %copy-done, bf16[4,2,128,128]{3,2,1,0:T(8,128)(2,1)S(1)} %copy-done.1, bf16[4,2,128,128]{3,2,1,0:T(8,128)(2,1)S(1)} %copy-done.2, ...), custom_call_target="tpu_custom_call" | custom-call | flops 4294967296 | bytes 1572864 | tf_op jit(solution)/shard_map/newton_step/pallas_call | solution.py:430
  67.0 0.7 %copy.11 = bf16[4,2,128,128]{3,2,1,0:T(8,128)(2,1)} copy(bf16[4,2,128,128]{3,2,1,0:T(8,128)(2,1)S(1)} %get-tuple-element.6) | data formatting | bytes 524288
  67.7 0.7 %copy.12 = bf16[4,2,128,128]{3,2,1,0:T(8,128)(2,1)} copy(bf16[4,2,128,128]{3,2,1,0:T(8,128)(2,1)S(1)} %get-tuple-element.7) | data formatting | bytes 524288
  68.4 0.7 %copy.13 = bf16[4,2,128,128]{3,2,1,0:T(8,128)(2,1)} copy(bf16[4,2,128,128]{3,2,1,0:T(8,128)(2,1)S(1)} %get-tuple-element.8) | data formatting | bytes 524288
Async XLA Ops:
  0.6 0.7 copy-start.4
  0.6 0.7 copy-start.3
  1.3 0.9 %copy-start = (bf16[4,2,128,128]{3,2,1,0:T(8,128)(2,1)S(1)}, bf16[4,2,128,128]{3,2,1,0:T(8,128)(2,1)}, u32[]{:S(2)}) copy-start(bf16[4,2,128,128]{3,2,1,0:T(8,128)(2,1)} %refs_0_.1) | copy-start | bytes 786436
  2.3 0.9 %copy-start.1 = (bf16[4,2,128,128]{3,2,1,0:T(8,128)(2,1)S(1)}, bf16[4,2,128,128]{3,2,1,0:T(8,128)(2,1)}, u32[]{:S(2)}) copy-start(bf16[4,2,128,128]{3,2,1,0:T(8,128)(2,1)} %refs_1_.1) | copy-start | bytes 786436
  3.2 0.9 %copy-start.2 = (bf16[4,2,128,128]{3,2,1,0:T(8,128)(2,1)S(1)}, bf16[4,2,128,128]{3,2,1,0:T(8,128)(2,1)}, u32[]{:S(2)}) copy-start(bf16[4,2,128,128]{3,2,1,0:T(8,128)(2,1)} %refs_2_.1) | copy-start | bytes 786436

commit v2 on v1

--- a/solution.py
+++ b/solution.py
@@ -89,7 +89,7 @@
         self.put(name, name[0], link, got, senders, receivers)
 
 
-def within(area, row, low, high):
+def within(area, low, high):
     first, end = max(area[1], low), min(area[1] + area[2], high)
     return (area[0], first, end - first) if end > first else None
 
@@ -142,17 +142,18 @@
         t.add(("H", "Xpz", j), "P", some(low, (2, 3), 2), True)
         t.relay(("H", "Xcpo", j), "c", ("H", "Xpo", j))
         t.relay(("H", "Xcpz", j), "c", ("H", "Xpz", j))
-        t.relay(("H", "Xzpo", j), "z", ("H", "Xpo", j), EVERY, lambda area: within(area, j, HALF, SPAN))
+        t.relay(("H", "Xzpo", j), "z", ("H", "Xpo", j), EVERY, lambda area: within(area, HALF, SPAN))
         t.relay(("H", "Xczpo", j), "c", ("H", "Xzpo", j))
         if j < 3:
             t.add(("H", "mo", j), "m", {r: rect(j, pick(r, range(HALF) if r < 2 else high)) for r in EVERY})
             t.relay(("H", "cmo", j), "c", ("H", "mo", j))
-            t.relay(("H", "zmo", j), "z", ("H", "mo", j), (0, 1), lambda area: within(area, j, area[0] - HALF + 1, SPAN))
+            t.relay(("H", "zmo", j), "z", ("H", "mo", j), (0, 1), lambda area: within(area, area[0] - HALF + 1, SPAN))
             t.relay(("H", "czmo", j), "c", ("H", "zmo", j))
-            t.add(("H", "Xmo", j), "M", some(range(1, HALF), (0, 1)), True)
+            t.add(("H", "Xmo", j), "M", some(range(HALF), (0, 1)), True)
             t.add(("H", "Xmz", j), "M", some(high, (0, 1), 2), True)
-            t.add(("H", "Xml", j), "m", some(range(0, 3 - j), (0, 1)), True)
-            for end in ("mo", "mz", "ml"):
+            t.relay(("H", "Xzmo", j), "z", ("H", "Xmo", j), EVERY, lambda area: within(area, 0, area[0] - HALF + 3 - j))
+            t.relay(("H", "Xczmo", j), "c", ("H", "Xzmo", j))
+            for end in ("mo", "mz"):
                 t.relay(("H", "Xc" + end, j), "c", ("H", "X" + end, j))
 
         core = 0 if j in (0, 3) else 1
@@ -160,7 +161,7 @@
         t.add(("P", "p", j), "p", {core: wide, 2 + core: few})
         t.relay(("P", "cp", j), "c", ("P", "p", j))
         t.add(("P", "Xp", j), "P", {2 + core: wide}, True)
-        t.add(("P", "Xq", j), "p", {2 + core: few}, True)
+        t.relay(("P", "Xq", j), "z", ("P", "Xp", j), EVERY, lambda area: within(area, HALF, SPAN))
         if j < 3:
             few, wide = rect(j, range(0, 3 - j)), rect(j, range(1, NS - 1 - j))
             t.add(("P", "m", j), "m", {core: few, 2 + core: wide})
@@ -175,6 +176,7 @@
 
 
 TABLE = build_table()
+NAMES = tuple(TABLE.rows)
 
 
 def view(refs, array, area):
@@ -221,26 +223,267 @@
         self.copy(row, sender).wait_recv()
         return True
 
-    def send(self, array, *ends):
-        for j in range(ROWS):
-            for end in ends:
-                self.send_one((array, end, j))
-
-    def recv(self, array, *ends):
-        for j in range(ROWS):
-            for end in ends:
-                self.recv_one((array, end, j))
-
-    def pass_on(self, array, end, *onward):
-        for j in range(ROWS):
-            if self.recv_one((array, end, j)):
-                for then in onward:
-                    self.send_one((array, then, j))
+    def play(self, step):
+        for entry in PLANS[self.kind, self.role][step]:
+            name = NAMES[abs(entry) - 1]
+            if entry > 0:
+                self.recv_one(name)
+            else:
+                self.send_one(name)
 
     def drain(self):
         for row in TABLE.rows.values():
             if self.kind in row.senders and self.role in row.areas:
                 self.copy(row, self.role).wait_send()
+
+
+PLANS = {
+    (0, 0): (
+        (-309, -310, -1, -2, -5, -78, -79, -82, -170, -261, -263, -11, -88, -179, -266, -268, -47, -132, -223,
+         -290, -293, 310, -173, 2, 79, 170, 261, 11, 88, 179, -169, 266, -14, 47, 309, -311, 132, 223, 290,
+         -260, 263, -264, 1, -3, 5, -8, 268, -269, -10, 293, -294, 78, -80, 82, -85, -19, 311, -96, -6, 84,
+         169, -171, 173, -176, 3, 8, -87, 175, 260, -262, 14, -17, -83, 264, -174, 93, 184, 80, -178, 85, -91,
+         19, -20, 269, 171, -265, 176, -182, 96, -97, 10, -187, -12, 6, -9, 262, 17, -15, 87, -270, -89, 83,
+         -86, 178, -180, 174, 9, -177, 20, -272, 138, -92, 97, 91, -94, 12, 94, -183, 188, 182, -185, 187,
+         -188, 89, -58, 271, 15, -18, 270, -271,),
+        (180, -68, -291,),
+        (265, 267, 49, -267,),
+        (21, 185, 229, 92, -71, -22, -95,),
+        (183, -186, -147, 59, 294, -303, 58, -59, -60, -238, 22, 98, 51, -99, 68, -69, 18, 189, 99, -190, 272,
+         -273, 148, 71, -72, 239, 48, -49, 147, -148, -149, 190, 238, -239, -240, 158, -50, 133, -134, 224,
+         -225, 273,),
+        (230, 303, -304, -135, -231,),
+        (-226,),
+        (162, 253, 55,),
+        (140, 50, 231, -51, 295, -296, 249, 135, 296, -136, 226, -227,),
+        (),
+        (),
+    ),
+    (0, 1): (
+        (-310, -2, -79, -170, -261, -11, -88, -179, -266, -47, -132, -223, -290, -309, -1, -5, -81, -172, -78,
+         310, 2, -263, 79, 170, 261, 11, 88, 179, 266, 47, -90, 132, 223, 290, -181, -82, 311, -268, -173,
+         309, -311, 81, 264, -84, 3, 8, -169, -14, 269, 1, -3, 5, -8, 172, 294, -175, 80, 85, -260, 263, -264,
+         -19, -6, 90, -93, -137, 171, 176, -10, 181, -184, 78, -80, -96, 82, -85, 262, -87, 17, -91, 268,
+         -269, 169, -171, -187, 173, -176, 260, -262, -270, 14, -17, 20, 6, -9, -178, 19, -20, 137, -138, 97,
+         12, -265, 9, -182, -228, 96, -97, 89, -58, 10, -12, -293, 91, 86, -94, -98, 187, -188, 180, 177,
+         -189, 87, -89, 270, -271, -272, 178, -180, -15, 94, -133, 265, -267, -224, 48, -49, -50, 185, -147,
+         188, 182, -185, 228, -229, 18, -291, -238, 271,),
+        (58, 293, -59, -60, -294,),
+        (21, 50, 267, -157, -22, -51,),
+        (15, 98, 22, -18, -99,),
+        (95, 186, 147, -148, -149, -161, 59, 238, -239, -240, 99, -252, 69, 190, -248, 189, -190, 157, 273,
+         -158, 72, 272, -273,),
+        (49, 148,),
+        (161, 252, 239, -162, -253,),
+        (54, 134, -55,),
+        (225, 139, -140, 304, 231, 230, -231, 248, -249, 295, -296, 51, 296, 136, 227,),
+        (),
+        (),
+    ),
+    (0, 2): (
+        (-309, -310, -1, -2, -4, -5, -78, -79, -81, -82, -170, -261, -11, -88, -179, -266, -47, -132, -223,
+         -290, -169, 310, -172, -173, 2, 79, 170, 261, 11, 88, 179, -260, 266, -14, 47, 309, -311, 132, 223,
+         290, -263, -91, 1, -3, 4, 5, -7, -8, -13, -6, 78, -80, 81, 82, -84, -85, -83, 311, 173, -176, -10,
+         172, -175, 8, 3, -87, 7, 17, -90, -182, 169, -171, 14, -17, 80, 59, -178, 260, -262, 263, 91, -264,
+         -94, -270, -174, 84, 10, -12, 13, 6, -9, -16, -15, 83, -86, -58, -147, 171, 182, -185, 175, -181, 87,
+         -89, 90, -93, 262, 9, -268, 264, 270, -271, -265, 174, -177, -21, 86, 97, -92, 12, 15, -18, 178,
+         -180, -183, 89, 58, -59, 16, -228, 265, -267, -238, 147, 93, -148, 181, -184, -98, 188, -293, 268,
+         -269, -189, 272, -273, 180, 177, -272, 267, 92, -95, 18, 99, 228, 183, 271, -186, -229,),
+        (238, -48, -239,),
+        (184, 190,),
+        (273, 291, 293, -133, -292, -294,),
+        (95, 269, 53, 134, -71, -303, -224, -230,),
+        (186, 225, 60, -61,),
+        (138, 292,),
+        (158, 61, 229,),
+        (162, -295, 150, 294, 303, -304, 249, 241, 149, -150, 253, 240, -241,),
+        (71, -72,),
+        (),
+    ),
+    (0, 3): (
+        (-310, -2, -79, -170, -261, -11, -88, -179, -266, -47, -132, -223, -290, -309, -1, -4, -5, -14, 310,
+         2, 79, 170, -58, 261, 11, 88, 179, -81, 266, 47, 132, 223, 290, -78, 311, -169, 309, -311, 3, 5, -8,
+         -260, 7, -172, 8, 1, -3, 4, 14, -7, -17, 80, 84, -263, -6, 85, 78, -80, 58, -59, 81, 176, -84, -83,
+         175, -96, 171, 17, -10, -13, 262, -87, 264, -90, 94, 169, -171, 172, -175, 12, -178, 9, -187, 16,
+         260, -262, 263, 6, -9, -264, 86, -265, -174, 96, 83, -86, -97, -48, 10, -12, 185, -15, 89, 93, -270,
+         87, -89, 13, -16, 271, -181, 90, -93, 177, -21, 187, -188, 18, -98, -268, 180, -92, 178, -180, 59,
+         -52, 267, 174, -177, -183, 265, -267, 148, 15, 184, -18, -137, 98, -99, 270, -271,),
+        (269, 189, 273, 181, -184, -189, -190, -228,),
+        (272, -157, -161, -273, -293,),
+        (95, 133, 268, 52, 92, 186, 229, -248, -252, -95, -269, -272, -53, -134,),
+        (224, 183, 239, -186, -225,),
+        (291, 137, -138, -292,),
+        (60, 292, 228, 294, 157, -158, -54, -61, -139, -229,),
+        (161, 293, 149, -162, -150, -230, -294,),
+        (61, 248, 240, -249, -241, -295, 252, -253, 304, 150, 241,),
+        (72,),
+        (),
+    ),
+    (1, 0): (
+        (-309, -310, -1, -2, -5, -78, -79, -82, -170, -261, -11, -88, -179, -266, -47, -132, -223, -290, 310,
+         -173, 2, 79, 170, 261, 11, 88, 179, -169, 266, -14, 47, 309, -311, 132, 223, 290, -91, 263, -264, 1,
+         -3, 268, -269, -6, 293, -294, 78, -80, -83, 311, -182, 84, 169, -171, 3, -174, 175, 260, -262, -260,
+         264, 10, -12, 93, -10, 87, -89, 184, -87, 19, -20, 269, -178, 96, -97, 80, -265, 30, -31, 171, -272,
+         -291, 20, -15, 138, 31, -92, 97, 262, -58, 188, 187, -188, 112, -147, 271, 111, -112, 203, -238, 33,
+         -34, 229, 36, -41, 270, -271, 114, -115, -42, 294, 34, 51, 12,),
+        (37, 202, 68, 205, -69, -71, -203, -206, -44, -45, 118, 89, -126, -127,),
+        (41, 178, -180, -183, 119, -129, -130, 209, -217, -218, 265, -267, 210, -220, -221, 180,),
+        (21, -22, 98, -99, 158, 44, 126, 303, -304, 217, 267,),
+        (189, -190, 22, 272, -273, 50, -51, 48, -49, 249, 99, 135, -136, 64, -65, 226, -227, 133, -134, 74,
+         -77, 153, -154, 224, -225, 230, -231, 190, 168, 244, -245, 273,),
+        (295, 49, -296,),
+        (),
+        (),
+        (259, 55, 65, 140, 231, 296,),
+        (),
+        (),
+    ),
+    (1, 1): (
+        (-310, -2, -79, -170, -261, -11, -88, -179, -266, -47, -132, -223, -290, -309, -1, -5, -78, 310, 2,
+         79, 170, 261, 11, 88, 179, 266, 47, 132, 223, 290, -169, 311, -260, 309, -311, 81, 264, -84, 3, -10,
+         269, 1, -3, 172, 294, -175, 80, -87, 263, -264, -178, 90, -93, -6, 171, -82, 181, -184, 262, -173,
+         268, -269, 12, -14, 78, -80, 89, -91, 169, -171, 20, -182, 19, -20, 137, -138, 97, -58, 30, -31, 96,
+         -97, 31, -265, 260, -262, 187, -188, -98, 111, -112, -189, 270, -271, 202, -203, -272, -133, 228,
+         -229, -224, 188, 293, -294, 33, -34, 112, -291, -147, 34, -238, 50, -51, 10, -12, 41, -15, 271,),
+        (115, 36, 87, -89, -41, -42,),
+        (-161, 69, 203, 206, 178, -180, 44, 126, 180,),
+        (157, 129, 37, -158, -252, -44, -45, 217, 267, 118, 220, -126, -127, 209, -217, -218, 22, 265, -267,),
+        (99, 21, -22, 304, 248, -249, 98, 190, -99, 273, 51, 49, 136, 65, 227, 134, 77, 154, 189, 225, -190,
+         164, -168, 231, 272, -273,),
+        (48, -49,),
+        (),
+        (255, 54, 245, -259, -55,),
+        (64, -65, 139, 296, -140, 230, -231, 295, -296,),
+        (),
+        (),
+    ),
+    (1, 2): (
+        (-309, -310, -1, -2, -5, -23, -78, -79, -82, -100, -170, -261, -11, -88, -179, -266, -47, -132, -223,
+         -290, -169, 310, -173, -191, 2, 79, 170, 261, -14, 11, 88, 179, -260, 266, -274, 47, 309, -311, 132,
+         223, 290, -10, -91, 1, -3, 4, -7, -87, -6, -35, 78, -80, 81, -84, 24, -29, -83, -116, 102, 311, -110,
+         -182, -207, 172, -175, 3, 7, -30, 169, -171, -174, -282, 193, -201, 80, 29, 263, -264, -58, -56, 62,
+         -66, 84, 13, -16, -147, -141, 171, -238, -232, 262, 110, -297, 175, -111, 12, 201, 90, -93, 25, -32,
+         89, 264, -33, 260, 66, 181, -262, -184, 180, 270, -271, 103, 10, -113, -12, -114, 32, 268, -269, -15,
+         87, -89, 228, -229, -275, 194, -204, 178, -180, 151, -155, 155, -92, 265, -267, 97, -202, 242, 272,
+         -273, -246, -183, -283, 291, -292, -205, 188, -298, -178, 271,),
+        (),
+        (-265,),
+        (267, 16, -70, -71, -21,),
+        (93, 99, 246, 184, 190, -98, 293, -294, -305, 269, 273,),
+        (53, 134, 67, 225, 42, -43, 292, 138, -189, 229, -272, 45, -46, 158, 43,),
+        (127, 294, -128, -48, 63, 130, -131, -67, 303, 249, -304, -64, 218, -219, 221, -222, -133, -153, 73,
+         -76, 46, -224, -230, 128,),
+        (219,),
+        (-244, 167, -295, 152, -156, 243, -247,),
+        (258,),
+        (),
+    ),
+    (1, 3): (
+        (-310, -2, -79, -170, -261, -11, -88, -179, -266, -47, -132, -223, -290, -309, -1, -5, -23, -14, 310,
+         2, 79, 170, 261, 11, 88, 179, 266, 47, 132, 223, -58, 290, -100, 311, 309, -311, 3, 7, -78, 1, -3, 4,
+         -7, 80, 84, -169, 78, 29, -80, -6, 24, -29, -101, 81, 110, -84, 175, -30, 169, -171, 171, -260, 260,
+         201, -262, 102, -110, 264, -111, 10, 66, 172, -175, -12, 193, -201, 16, -202, -83, 87, -89, 263,
+         -264, 62, -66, -174, 178, -180, -191, -15, 25, -32, -192, 93, -33, -92, 32, -274, 262, 184, 151,
+         -155, 271, -10, 96, 113, -97, 12, -183, -275, 269, -87, 89, 187, 229, -188, -35, 204, 180, 270, -271,),
+        (155,),
+        (267, 13, 265, 273, 246, 242, 98, 292, 90, -159, -161, -178, -267, -16, -93, -99, -246,),
+        (189, 181, -184, -190,),
+        (272, 268, -269, -273,),
+        (133, 52, -53, -134, 63, 224, -67, -225, -265, 291, -292, 137, -138, -252, 294, -21, 228, -229, 157,
+         -158, 42, -43, 43, 293, -294, -250, 248, -249, -98, 46,),
+        (-116, 128, 131, 67, -117, 304, 45, -46, -207, 219, 127, 222, -128,),
+        (-208, 218, -219,),
+        (-189, -282, 76, -283, 163, -167, -272, -56, -48, -141, -142, -54, -232, -64, -139, 156, -233, 247,),
+        (-230, -297, 254, -258, -295, -298,),
+        (),
+    ),
+    (2, 0): (
+        (-309, -310, -1, -2, -24, -78, -79, -102, -170, -261, -263, -11, -88, -179, -266, -268, -47, -132,
+         -223, -290, -293, 310, -193, 2, 79, 170, 261, 11, 88, 179, -169, 266, -62, 47, 309, -311, 132, 223,
+         290, -260, 1, -3, 5, -8, -10, 78, -80, 82, -85, 23, -19, -26, 311, 100, -96, -104, -27, -25, 173,
+         -176, 3, 8, -105, 169, -171, 14, -17, -103, 191, -187, -195, 80, -196, 26, 274, -276, -194, 171, 85,
+         -277, -151, 262, -87, 176, -242, 260, -262, 6, 104, -9, 12, -178, 17, -36, 10, -270, -12, 83, -86,
+         87, -89, 174, 9, -177, -265, 107, -37, 56, -57, 91, -94, -291, 89, 94, -118, 141, -143, 182, -185,
+         180, 232, -234, 15, -18, -119, 178, -180, 267, 49, 297, -299, -209, 265, -267, -210, 39, -40, 185,
+         92, -95, 121, -122, 183, 195, -186, -301, 59, 212, 275, 198, -279, -213, 58, -59, 285, -286, 276, 18,
+         48, -49, -50, -63, 279,),
+        (133, 298, 148, 224, -68, -73, -280, -134, -225, -300,),
+        (71, 239, -72,),
+        (147, -148,),
+        (238, -303, -239, 288, -289, 165, 70, -74, -75, 40, 162, -152, 253, -135, -243, -60, -149, 305, -307,
+         -306, -240, -226, 256, 122, 125, 57, 213, 143, 216, 144, 286, 234, 289,),
+        (),
+        (235,),
+        (299,),
+        (300,),
+        (),
+        (),
+    ),
+    (2, 1): (
+        (-310, -2, -79, -170, -261, -11, -88, -179, -266, -47, -132, -223, -290, -309, -1, -24, -81, -172,
+         -78, 310, 2, -263, 79, 170, 261, 11, 88, 179, 266, 47, -90, 132, 223, 290, -181, -102, 311, -268,
+         -193, 309, -311, 3, 8, -169, -62, 1, -3, 5, -8, 80, 85, 78, -80, 26, 23, -19, -26, -25, 104, 176,
+         169, -171, 82, -85, -151, -96, 171, 17, -27, 260, -262, 173, 195, -176, 100, -104, -187, 10, -12, 14,
+         276, -17, -270, -137, 6, -9, 262, -105, 9, -242, 101, -107, -228, 12, -36, 87, -89, -293, 91, 86,
+         -94, 89, 177, -108, 178, -180, -260, 265, -267, 48, -49, -50, 57, -10, 94, -63, 143, -87, 185, 182,
+         -185, 234, -178, 18, 191, -195, 180, 58, -59, 299, -196, -37, 192, -198, 267, -118, 274, -276, 40,
+         15, -199, -18, -209, 95, 122, 186, -277, 275, -279, 147, 279, -280, -148,),
+        (213, 59, 286, 238, -265, -239,),
+        (49,),
+        (-157, -60,),
+        (134, -163, -133, 225, 300, 159, -165, -160, -149, 72, 39, -40, 161, 148, -162, -224, 252, -253, 239,
+         -240, 289, -291, 75, -164, -248, -254, 307, -255, 250, -251, -256, 121, -122, 124, -125, 56, -57,
+         212, -213, 141, -143, -145, 215, -216, 142, -144, 285, -286, 232, -234, -236, 288, -289,),
+        (233, -235,),
+        (297, -299, -301,),
+        (298, -300,),
+        (),
+        (),
+        (),
+    ),
+    (2, 2): (
+        (-309, -310, -1, -2, -4, -78, -79, -81, -170, -261, -11, -88, -179, -266, -47, -132, -223, -290, 310,
+         -172, 2, 79, 170, 261, 11, 88, 179, -169, 266, -263, 47, 309, -311, 132, 223, 290, -13, 1, -3, 5, -8,
+         -90, 78, -80, 82, -85, 311, 173, -176, -260, 8, 3, 17, -10, 169, -171, 14, -17, -181, 80, 59, -87,
+         260, -262, 91, -94, 10, -12, 6, -9, -270, 83, -86, -268, 27, -28, 35, -38, 171, 182, -185, -228, 105,
+         -106, 116, -178, -120, -293, 9, 196, -197, 207, -265, -211, 174, -177, 86, -39, 15, -18, 282, -284,
+         277, -278, -121, 28, 58, -59, 87, -89, -212, 147, -148, 178, -180, -285, -48, 265, -267, 177, -133,
+         106, 291, -292, 18, -224, 92, -95, 109, 95, 183, -186, 262, 238, -239, 12, 186, 89, 283, -287, -288,
+         301, -302, 180, 38, 197, 200, 278, 280, -281, 281,),
+        (),
+        (267,),
+        (),
+        (61, 134, -303, 166, 162, 150, 225, 60, -61, 241, 149, 253, -150, 292, 71, -72, 306, -308, 120, 240,
+         -241, 123, 211, 214, 257, 284, 287,),
+        (),
+        (),
+        (),
+        (146, 237, 302,),
+        (),
+        (),
+    ),
+    (2, 3): (
+        (-310, -2, -79, -170, -261, -11, -88, -179, -266, -47, -132, -223, -290, -309, -1, -4, -78, 310, 2,
+         79, 170, 261, 11, 88, 179, 266, 47, 132, 223, 290, -169, 311, -260, 309, -311, 3, 5, -8, -10, 8, -81,
+         1, -3, 14, -17, 80, 85, -172, 78, -80, 58, -59, -96, 176, -263, 171, 17, -87, 262, 94, -178, -13,
+         169, -171, 12, 9, -265, 6, -9, 86, -48, 28, 83, -86, 38, 185, -187, 106, 120, 27, -28, -90, 197, 211,
+         177, -181, 18, -268, 284, 278, 59, -52, 89, 174, -177, -137, 105, -106, 148, 180, 15, -18, -228, 108,
+         -109, 92, -95, -293, 267, 260, -262, -270, 292, 10, -12, 95, 183, -186, 87, -89, 186, 178, -180, 35,
+         -38, -39, 239, 196, -197, 287, 199, -200, 302, 277, -278, 280, -281, 265, -267, 60, -61, 133, 281,
+         -134,),
+        (160, -166,),
+        (149, 161, -157, -162, -150,),
+        (224, -248, -225,),
+        (240, -241, 252, -253, 291, -292, 116, -120, -121, 117, -123, -124, 61, 150, 207, -211, -212, 208,
+         -214, -215, 251, -257, 72, 308, 241, 282, -284, -285, 283, -287, -288,),
+        (),
+        (),
+        (),
+        (145, -146, 236, -237, 301, -302,),
+        (),
+        (),
+    ),
+}
 
 
 def kernel(panels, root_in, inverse_in, hamilton_in, margin_in, hamilton_mask_in,
@@ -300,33 +543,6 @@
                 def _():
                     plan(Role(kind, role, refs, send_sem, recv_sem, cannon, panels))
 
-    def gather(d):
-        d.send("R", "zo", "co")
-        d.send("R", "po", "mo", "Xpo", "Xmo")
-        d.send("M", "zo", "co")
-        d.send("I", "zo", "co")
-        d.pass_on("R", "zo", "cz", "pz", "mz", "Xpz", "Xmz")
-        d.send("I", "po", "mo", "Xpo", "Xmo")
-        d.pass_on("M", "zo", "cz")
-        d.pass_on("R", "po", "cpo")
-        d.pass_on("R", "mo", "cmo")
-        d.send("H", "zo", "co", "po", "mo", "Xpo", "Xmo", "Xml")
-        d.pass_on("I", "zo", "cz", "mz", "Xmz", "Xpz")
-        d.pass_on("R", "pz", "cpz")
-        d.pass_on("R", "mz", "cmz")
-        for end in ("po", "mo", "pz", "mz"):
-            d.pass_on("R", "X" + end, "Xz" + end, "Xc" + end)
-        d.pass_on("I", "po", "cpo", "zpo")
-        d.pass_on("H", "zo", "cz", "pz", "Xpz", "Xmz")
-        for end in ("po", "mo", "pz", "mz"):
-            d.pass_on("R", "Xz" + end, "Xcz" + end)
-        d.recv("M", "co", "cz")
-        d.recv("I", "co", "cz")
-        d.recv("R", "co", "cz", "cpo", "cpz", "cmo", "cmz")
-        for end in ("po", "mo", "pz", "mz"):
-            d.recv("R", "Xc" + end, "Xcz" + end)
-
-    by_role(gather)
 
     def mask_row(i):
         return jnp.concatenate([margin[(t // 2) * 8 + i * 2 + t % 2:(t // 2) * 8 + i * 2 + t % 2 + 1, :]
@@ -340,68 +556,32 @@
 
     at_row = lax.broadcasted_iota(jnp.int32, (BLK, NS * BLK), 0)
     at_col = lax.broadcasted_iota(jnp.int32, (BLK, NS * BLK), 1)
-    diagonal = jnp.where(at_col - HALF * BLK == at_row, 1.5, 0.0).astype(jnp.float32)
     for i in range(ROWS):
+        by_role(lambda d: d.play(i))
         product = jnp.dot(inverse[own(i), window(i)], root[window(i), window(i)], preferred_element_type=jnp.float32)
+        diagonal = jnp.where(at_col - HALF * BLK == at_row, 1.5, 0.0).astype(jnp.float32)
         poly[own(i), window(i)] = (diagonal - 0.5 * (product * mask_row(i))).astype(jnp.bfloat16)
 
-    def exchange(d):
-        d.send("P", "p", "m", "Xp", "Xq", "Xm", "Xn")
-        d.pass_on("I", "mo", "cmo")
-        d.pass_on("I", "mz", "cmz")
-        for end in ("po", "mo", "pz", "mz"):
-            d.pass_on("I", "X" + end, "Xz" + end, "Xc" + end)
-        d.pass_on("I", "zpo", "czpo")
-        d.pass_on("H", "po", "cpo", "zpo")
-        d.pass_on("H", "mo", "cmo", "zmo")
-        d.pass_on("H", "pz", "cpz")
-        for end in ("po", "mo", "pz", "mz"):
-            d.pass_on("I", "Xz" + end, "Xcz" + end)
-        d.recv("I", "cpo", "cmo", "cmz", "czpo")
-        for end in ("po", "mo", "pz", "mz"):
-            d.recv("I", "Xc" + end, "Xcz" + end)
-
-    by_role(exchange)
-
     for i in range(ROWS):
+        by_role(lambda d: d.play(ROWS + i))
         product = jnp.dot(poly[own(i), window(i)], inverse[window(i), window(i)], preferred_element_type=jnp.float32)
         next_rows[i] = (product * mask_row(i)).astype(jnp.bfloat16)
         mine = next_rows[i, :, pl.ds(pl.multiple_of(2 * rep * BLK, 2 * BLK), 2 * BLK)]
         for b in range(2):
             inverse_out[i, b] = mine[:, b * BLK:(b + 1) * BLK]
 
-    def settle(d):
-        d.pass_on("H", "zpo", "czpo")
-        d.pass_on("H", "zmo", "czmo")
-        d.pass_on("H", "Xpo", "Xzpo", "Xcpo")
-        d.pass_on("H", "Xpz", "Xcpz")
-        for end in ("mo", "mz", "ml"):
-            d.pass_on("H", "X" + end, "Xc" + end)
-        d.pass_on("H", "Xzpo", "Xczpo")
-        d.pass_on("P", "p", "cp")
-        d.pass_on("P", "m", "cm")
-        for end in ("q", "n", "p", "m"):
-            d.pass_on("P", "X" + end, "Xc" + end)
-        d.recv("H", "co", "cz", "cpo", "cpz", "cmo", "czpo", "czmo")
-        d.recv("H", "Xcpo", "Xcpz", "Xczpo", "Xcmo", "Xcmz", "Xcml")
-
-    by_role(settle)
-
     def narrow(first, second, i):
         cols = pl.ds(pl.multiple_of((i + 2 * rep) * BLK, BLK), 2 * BLK)
         return jnp.dot(first, second[window(i), cols], preferred_element_type=jnp.float32)
 
+    by_role(lambda d: d.play(2 * ROWS))
     for i in range(ROWS):
         product = narrow(next_rows[i], hamilton, i)
         for b in range(2):
             keep = hamilton_mask_in[b, i].astype(jnp.float32)
             lowdin_out[i, b] = (product[:, b * BLK:(b + 1) * BLK] * keep).astype(jnp.bfloat16)
 
-    def last(d):
-        d.recv("P", "cp", "cm", "Xcp", "Xcq", "Xcm", "Xcn")
-
-    by_role(last)
-
+    by_role(lambda d: d.play(2 * ROWS + 1))
     for i in range(ROWS):
         product = narrow(root[own(i), window(i)], poly, i)
         for b in range(2):
@@ -409,6 +589,7 @@
             root_out[i, b] = (product[:, b * BLK:(b + 1) * BLK] * keep).astype(jnp.bfloat16)
 
     def finish(d):
+        d.play(2 * ROWS + 2)
         d.drain()
 
     by_role(finish)

time: 69.8 us -> 81.3 us (1.16)
  Pallas kernels: 62.8 us -> 74.8 us
    pallas_call x1, Pallas kernels: 62.8 us -> 74.8 us  [body(): pl.pallas_call(run, out_shape=(shape, shape, shape), in_specs=[vmem, vmem...]
where the time goes in v2:
time: 81.3 us; the launch traced here: 81.1 us
  Pallas kernels  74.8 us (92%)
  local copies, waits for them, and re-layouts  5.64 us (7%)
    pallas_call x1, Pallas kernels, body(): pl.pallas_call(run, out_shape=(shape, shape, shape), in_specs=[vmem, vmem...  74.8 us
    unnamed x13, local copies, waits for them, and re-layouts  5.64 us

profile of v2, /device:TPU:1, one launch (start us, length us, event | category | flops | bytes accessed | tf_op | source)
XLA Modules:
  0.0 81.1 jit_solution(8599706015446053440)
XLA Ops:
  0.6 0.0 copy-start.4
  0.6 0.0 copy-start.3
  0.7 0.7 copy-done.4
  1.3 0.0 copy-done.3
  1.3 0.0 copy-start
  1.3 0.9 %copy-done = bf16[4,2,128,128]{3,2,1,0:T(8,128)(2,1)S(1)} copy-done((bf16[4,2,128,128]{3,2,1,0:T(8,128)(2,1)S(1)}, bf16[4,2,128,128]{3,2,1,0:T(8,128)(2,1)}, u32[]{:S(2)}) %copy-start) | copy-done | bytes 262168
  2.3 0.0 copy-start.1
  2.3 0.9 %copy-done.1 = bf16[4,2,128,128]{3,2,1,0:T(8,128)(2,1)S(1)} copy-done((bf16[4,2,128,128]{3,2,1,0:T(8,128)(2,1)S(1)}, bf16[4,2,128,128]{3,2,1,0:T(8,128)(2,1)}, u32[]{:S(2)}) %copy-start.1) | copy-done | bytes 262168
  3.2 0.0 copy-start.2
  3.2 0.9 %copy-done.2 = bf16[4,2,128,128]{3,2,1,0:T(8,128)(2,1)S(1)} copy-done((bf16[4,2,128,128]{3,2,1,0:T(8,128)(2,1)S(1)}, bf16[4,2,128,128]{3,2,1,0:T(8,128)(2,1)}, u32[]{:S(2)}) %copy-start.2) | copy-done | bytes 262168
  4.2 74.8 %newton_step.1 = (bf16[4,2,128,128]{3,2,1,0:T(8,128)(2,1)S(1)}, bf16[4,2,128,128]{3,2,1,0:T(8,128)(2,1)S(1)}, bf16[4,2,128,128]{3,2,1,0:T(8,128)(2,1)S(1)}) custom-call(bf16[4,2,128,128]{3,2,1,0:T(8,128)(2,1)S(1)} %copy-done, bf16[4,2,128,128]{3,2,1,0:T(8,128)(2,1)S(1)} %copy-done.1, bf16[4,2,128,128]{3,2,1,0:T(8,128)(2,1)S(1)} %copy-done.2, ...), custom_call_target="tpu_custom_call" | custom-call | flops 4294967296 | bytes 1572864 | tf_op jit(solution)/shard_map/newton_step/pallas_call | solution.py:611
  79.0 0.7 copy.11
  79.7 0.7 copy.12
  80.4 0.7 copy.13
Async XLA Ops:
  0.6 0.7 copy-start.4
  0.6 0.7 copy-start.3
  1.3 0.9 %copy-start = (bf16[4,2,128,128]{3,2,1,0:T(8,128)(2,1)S(1)}, bf16[4,2,128,128]{3,2,1,0:T(8,128)(2,1)}, u32[]{:S(2)}) copy-start(bf16[4,2,128,128]{3,2,1,0:T(8,128)(2,1)} %refs_0_.1) | copy-start | bytes 786436
  2.3 0.9 %copy-start.1 = (bf16[4,2,128,128]{3,2,1,0:T(8,128)(2,1)S(1)}, bf16[4,2,128,128]{3,2,1,0:T(8,128)(2,1)}, u32[]{:S(2)}) copy-start(bf16[4,2,128,128]{3,2,1,0:T(8,128)(2,1)} %refs_1_.1) | copy-start | bytes 786436
  3.2 0.9 %copy-start.2 = (bf16[4,2,128,128]{3,2,1,0:T(8,128)(2,1)S(1)}, bf16[4,2,128,128]{3,2,1,0:T(8,128)(2,1)}, u32[]{:S(2)}) copy-start(bf16[4,2,128,128]{3,2,1,0:T(8,128)(2,1)} %refs_2_.1) | copy-start | bytes 786436

commit v3 on v1

--- a/solution.py
+++ b/solution.py
@@ -89,7 +89,7 @@
         self.put(name, name[0], link, got, senders, receivers)
 
 
-def within(area, row, low, high):
+def within(area, low, high):
     first, end = max(area[1], low), min(area[1] + area[2], high)
     return (area[0], first, end - first) if end > first else None
 
@@ -142,17 +142,18 @@
         t.add(("H", "Xpz", j), "P", some(low, (2, 3), 2), True)
         t.relay(("H", "Xcpo", j), "c", ("H", "Xpo", j))
         t.relay(("H", "Xcpz", j), "c", ("H", "Xpz", j))
-        t.relay(("H", "Xzpo", j), "z", ("H", "Xpo", j), EVERY, lambda area: within(area, j, HALF, SPAN))
+        t.relay(("H", "Xzpo", j), "z", ("H", "Xpo", j), EVERY, lambda area: within(area, HALF, SPAN))
         t.relay(("H", "Xczpo", j), "c", ("H", "Xzpo", j))
         if j < 3:
             t.add(("H", "mo", j), "m", {r: rect(j, pick(r, range(HALF) if r < 2 else high)) for r in EVERY})
             t.relay(("H", "cmo", j), "c", ("H", "mo", j))
-            t.relay(("H", "zmo", j), "z", ("H", "mo", j), (0, 1), lambda area: within(area, j, area[0] - HALF + 1, SPAN))
+            t.relay(("H", "zmo", j), "z", ("H", "mo", j), (0, 1), lambda area: within(area, area[0] - HALF + 1, SPAN))
             t.relay(("H", "czmo", j), "c", ("H", "zmo", j))
-            t.add(("H", "Xmo", j), "M", some(range(1, HALF), (0, 1)), True)
+            t.add(("H", "Xmo", j), "M", some(range(HALF), (0, 1)), True)
             t.add(("H", "Xmz", j), "M", some(high, (0, 1), 2), True)
-            t.add(("H", "Xml", j), "m", some(range(0, 3 - j), (0, 1)), True)
-            for end in ("mo", "mz", "ml"):
+            t.relay(("H", "Xzmo", j), "z", ("H", "Xmo", j), EVERY, lambda area: within(area, 0, area[0] - HALF + 3 - j))
+            t.relay(("H", "Xczmo", j), "c", ("H", "Xzmo", j))
+            for end in ("mo", "mz"):
                 t.relay(("H", "Xc" + end, j), "c", ("H", "X" + end, j))
 
         core = 0 if j in (0, 3) else 1
@@ -160,7 +161,7 @@
         t.add(("P", "p", j), "p", {core: wide, 2 + core: few})
         t.relay(("P", "cp", j), "c", ("P", "p", j))
         t.add(("P", "Xp", j), "P", {2 + core: wide}, True)
-        t.add(("P", "Xq", j), "p", {2 + core: few}, True)
+        t.relay(("P", "Xq", j), "z", ("P", "Xp", j), EVERY, lambda area: within(area, HALF, SPAN))
         if j < 3:
             few, wide = rect(j, range(0, 3 - j)), rect(j, range(1, NS - 1 - j))
             t.add(("P", "m", j), "m", {core: few, 2 + core: wide})
@@ -175,6 +176,7 @@
 
 
 TABLE = build_table()
+NAMES = tuple(TABLE.rows)
 
 
 def view(refs, array, area):
@@ -221,21 +223,13 @@
         self.copy(row, sender).wait_recv()
         return True
 
-    def send(self, array, *ends):
-        for j in range(ROWS):
-            for end in ends:
-                self.send_one((array, end, j))
-
-    def recv(self, array, *ends):
-        for j in range(ROWS):
-            for end in ends:
-                self.recv_one((array, end, j))
-
-    def pass_on(self, array, end, *onward):
-        for j in range(ROWS):
-            if self.recv_one((array, end, j)):
-                for then in onward:
-                    self.send_one((array, then, j))
+    def play(self, step):
+        for entry in PLANS[self.kind, self.role][step]:
+            name = NAMES[abs(entry) - 1]
+            if entry > 0:
+                self.recv_one(name)
+            else:
+                self.send_one(name)
 
     def drain(self):
         for row in TABLE.rows.values():
@@ -243,9 +237,263 @@
                 self.copy(row, self.role).wait_send()
 
 
-def kernel(panels, root_in, inverse_in, hamilton_in, margin_in, hamilton_mask_in,
+PLANS = {
+    (0, 0): (
+        (-309, -310, -1, -2, -5, -78, -79, -82, -169, -170, -173, -260, -261, -263, -10, -11, -88, -179, -266,
+         -14, -91, -268, -47, -132, -223, -290, -293, 310, 2, 79, 170, -87, 261, -182, 11, 88, 179, 266, 47,
+         132, 309, -311, 223, -178, -58, 290, 263, 1, -3, -264, -265, 5, -8, 268, -269, 293, 78, -80, -272,
+         -294, 82, -85, -19, -291, 169, -171, 173, -6, -176, -96, 84, 260, -262, 14, -83, -17, -187, 10, 175,
+         91, -12, -94, -270, 264, -174, 311, 93, -15, 182, -185, 3, -147, 184, 8, 87, -89, 58, -59, 80, -92,
+         269, 138, 178, -180, -60, 265, 229, -267, -183, 19, -20, 85, 48, 294, 6, -9, -49, -50, 96, -97, 176,
+         133, -134, -135, 83, -86, 187, 224, -188, -225, -226, -238, 270, -271, 174, -177, 21, -22, 15, -18,
+         17, 171, 147, -148, -149, 20, 50, 98, -99, -51, 92, -95, 97, 262, 135, -136, 183, -186, 226, -227,
+         189, -190, 9, 12, 94, 272, 188, 238, -273, -239, -240, 230, -231, 89, 185, 271,),
+        (-68, -71,),
+        (180,),
+        (59, 148, 295, -296, 267,),
+        (18, 22, 239, -303, 99, 71, -72, 162, 190, 273,),
+        (68, -69,),
+        (158, 253, 49, 55,),
+        (140,),
+        (231, 296, 249, 303, -304, 51,),
+        (),
+        (),
+    ),
+    (0, 1): (
+        (-310, -2, -79, -81, -170, -172, -261, -263, -11, -88, -179, -266, -90, -47, -132, -223, -290, -181,
+         -309, -1, -5, 310, 2, 79, -268, 170, 261, 11, 88, 179, 266, 47, 132, -137, 223, 290, -228, -82, 311,
+         -293, -173, 81, -84, 3, 264, 8, 269, -78, 172, -175, 80, 294, 85, -169, 263, -264, 171, 176, 90, 309,
+         -311, -260, -14, -93, 262, 17, 181, 1, -3, -10, -184, 5, -8, -19, 12, 94, 268, 78, -80, -87, -269,
+         137, -138, -96, -178, 228, -229, 185, 82, -85, 293, -294, -265, 89, -6, 59, 173, -176, -98, 180, -91,
+         -189, 267, -182, 20, -272, 9, 49, 97, 14, -17, -133, 169, -171, -187, -58, -224, 134, 86, 188, 225,
+         19, -20, -291, -147, 271, 177, 96, 260, -97, -262, -270, -238, 22, 18, 6, -9, 148, 10, -12, -15, 99,
+         51, 95, 91, -94, 187, -188, 136, 186, 227, 87, -89, 182, -185, 270, -271,),
+        (190,),
+        (58, 178, 273, 239, 231, 147, -157, -161, -180, -59, -60, -148, -149,),
+        (265, 238, 21, 15, -248, -252, -267, -18, -22, -239, -240,),
+        (98, -99, 161, -162, 189, -190, 296, 272, -273,),
+        (157, 48, 252, 54, -158, -253, -49, -55,),
+        (72, 139, -50, -140,),
+        (230, 295, -231, -296,),
+        (69, 248, -249, 50, -51,),
+        (304,),
+        (),
+    ),
+    (0, 2): (
+        (-309, -310, -1, -2, -4, -5, -78, -79, -81, -82, -169, -170, -172, -173, -260, -261, -263, -10, -11,
+         -88, -179, -266, -13, -14, -91, -182, -47, -58, -132, -223, -290, 310, 2, 79, 170, 261, -90, -147,
+         11, 88, 179, 266, 47, 132, 309, -311, 223, -87, -181, -238, 290, 1, -3, -178, -268, 4, 5, -6, -7, -8,
+         78, -80, -265, -228, 81, 82, -83, -84, -85, 173, -176, -293, 169, -171, -48, 172, -174, -175, 14,
+         -17, 260, -262, -133, 263, -264, 91, -270, -94, 10, -12, -224, 13, 182, -15, -16, -185, 58, -59, 311,
+         -21, 87, -89, 90, 147, -92, -93, -148, 3, 238, -239, 7, 178, -180, 181, -184, -183, -98, 265, -267,
+         268, 6, -9, -269, 272, -273, 228, 8, -229, 291, -292, 83, -86, -189, 293, -294, 174, -177, 270, -271,
+         -272, 80, 15, -18, 84, 17, -230, 171, 59, 262, 175, 92, -95, 12, 9, 264, 183, -186, 60, -61, 89, 16,
+         -295, 180, 93, 86, 184, 267, 177, 99, 269, 97, 190, 18, 53, 273, 188, 95, 134, 271,),
+        (186, 149, 240, -71, -150, -241,),
+        (138, 225, 292,),
+        (229, 294,),
+        (-303,),
+        (61,),
+        (158, 71, 150, -72,),
+        (249, 241,),
+        (303, -304,),
+        (162, 253,),
+        (),
+    ),
+    (0, 3): (
+        (-310, -2, -79, -170, -261, -11, -88, -179, -266, -47, -132, -223, -290, -309, -1, -4, 310, 2, 79,
+         -78, 170, 261, 11, 88, 179, 266, 47, 132, 223, 290, -5, 311, 3, 7, 8, 80, -81, 84, 85, 176, -14, 171,
+         -58, 175, 309, -311, -172, 17, -169, 262, 264, 1, -3, 4, -7, -263, -6, 94, 12, 16, 185, -13, -260,
+         59, 5, -8, -90, 89, 93, 148, 239, -181, -10, 180, 184, -268, 267, 9, 269, 78, 273, -80, -83, -96,
+         229, 292, -87, 81, 14, 86, -84, -17, -52, 169, -171, -174, 58, 294, -187, -59, 177, 260, -262, 172,
+         -175, -270, 271, 10, -12, -178, -15, -137, 263, 6, -9, -264, 18, 87, -89, -265, -92, -228, 13, -16,
+         178, -180, -21, -183, -293, 90, -93, 95, 181, 83, -86, -184, 265, -267, 186, 98, 61, 268, 174, -177,
+         -98, -99, -269, 96, -97, 189, -189, -190, 52, 15, -18, -53, 272, -272, -273, 187, 92, -188, -95, 133,
+         -134, -48, 270, 183, -271, -186,),
+        (224, 137, 291, -54, -138, -139, -225, -292,),
+        (228, 293, -157, -161, -229, -230, -294, -295,),
+        (-248, -252,),
+        (150, 241, 60, -61,),
+        (157, 149, -158, -150,),
+        (240, 248, -249, -241,),
+        (),
+        (),
+        (161, 72, -162, 252, -253, 304,),
+        (),
+    ),
+    (1, 0): (
+        (-309, -310, -1, -2, -5, -78, -79, -82, -169, -170, -173, -260, -261, -10, -11, -88, -179, -266, -14,
+         -91, -47, -132, -223, -290, 310, 2, 79, 170, 261, 11, 88, 179, 266, 47, 132, 309, -311, 223, -87,
+         -182, 290, 263, 1, -3, -264, -178, 268, -269, 293, 78, -80, -265, -294, 169, -171, -272, -291, 84,
+         260, -262, -6, 10, 175, -12, 264, -83, 311, 93, -174, 3, -15, 184, 87, -89, 80, -92, 269, 138, 178,
+         -180, 36, -41, -183, 265, 229, -267, -42, -58, 118, -126, 19, -20, 294, -147, 96, -97, 187, -188,
+         -127, 171, -238, 270, -271, 262, 209, -217, 12, 89, 37, -44, 20, 50, -51, 180, 97, -45, 135, 30, -31,
+         -136, 267, 226, 49, -218, -227, 119, -129, 33, -34, -130, 111, -112, 210, -220, -221, 114, 188, -115,
+         202, 271, -203,),
+        (205, -71, -206, 31,),
+        (21, -22, 34, 112,),
+        (41, 44, 126, 203,),
+        (98, -99, 22, 189, -190, 217, 158, 68, -69, 272, -273, 99, 48, -49, 64, -65, 74, -77, 249, 190, 133,
+         -134, 303, -304, 273,),
+        (153, -154,),
+        (224, 230, 51, 55, -225, -231,),
+        (244, -245,),
+        (168, 65, 295, -296, 259, 140, 231, 296,),
+        (),
+        (),
+    ),
+    (1, 1): (
+        (-310, -2, -79, -170, -261, -11, -88, -179, -266, -47, -132, -223, -290, -309, -1, -5, 310, 2, 79,
+         170, -78, -82, 261, 11, 88, 179, 266, 47, 132, 223, 290, -173, 311, -14, 81, -84, 3, 264, 269, -91,
+         172, -175, 80, 294, -169, 263, -264, 171, 90, 309, -311, -260, -93, -182, 262, 181, 1, -3, -10, -184,
+         12, 268, 78, -80, -87, -269, 137, -138, -178, 228, -229, -265, 293, -294, 89, 180, 41, 169, -171,
+         -98, -189, 267, 126, 260, 20, -262, -6, 10, 97, -12, -272, -15, 87, 188, -89, -58, 19, -20, -133,
+         178, 271, -180, -147, -224, 217, 96, -97, 265, -267, -291, -238, 48, -49, 44, 51, 187, -188, 31, 136,
+         227, 129, 270, -271,),
+        (34, 112, 220, 115, 30, -31,),
+        (203, 33, 206, -161, -34, 111, -112,),
+        (36, 37, -252, -41, -42, -44, -45, 118, -126, -127, 202, -203,),
+        (209, 22, 21, -22, -217, -218, 157, -158, 98, -99, 99, 190, 69, 273, 248, -249, 189, -190, 49, 272,
+         -273,),
+        (65, 77,),
+        (54, 50, 134, -51, -55,),
+        (164, 64, 304, -168, -65,),
+        (154, 255, 139, -259, -140, 225, 231, 245, 230, -231, 295, 296, -296,),
+        (),
+        (),
+    ),
+    (1, 2): (
+        (-309, -310, -1, -2, -5, -23, -78, -79, -82, -100, -169, -170, -173, -191, -260, -261, -274, -10, -11,
+         -88, -179, -266, -14, -35, -91, -182, -47, -58, -132, -223, -290, 310, 2, 79, 170, 261, -147, 11, 88,
+         179, 266, 47, 132, 309, -311, 223, -87, -238, 290, -116, 1, -3, -178, 4, -6, -7, -207, 78, -80, -265,
+         81, -83, -84, -282, 24, -29, 169, -171, 172, -174, -175, -56, 102, -110, 260, -262, 263, -264, -275,
+         193, -201, 10, -12, 13, -15, -16, 62, -66, 151, -155, 311, -141, 90, -93, 242, -246, 3, -232, 7, 87,
+         -89, 181, -92, -184, 80, -297, 178, -180, 268, -183, -269, -30, 228, -229, 265, -267, 25, 272, -32,
+         -33, -273, 293, -294, 291, -292, 103, -113, -111, 194, -204, -114, 84, -202, 171, 175, -205, 262,
+         270, -271, 264, 29, -283, 12, 16, 89, 32, -21, 180, 93, 42, 110, -43, 267, 184, 269, 97, 201, 99,
+         127, -98, -128, 53, 190, 66, -189, 188, 63, -67, -298, 155, 271,),
+        (-70, -71, -272,),
+        (273, 134, 138, 45, -46, -48,),
+        (225, 218, 229, 246, 292, 294, 130, -131, -219, -64,),
+        (152, 221, 243, -222, -133, -156, -247,),
+        (158, -153, 67, -305, 249, 43,),
+        (303, -304, -224, -230, -244, 73, 46, 128, -76,),
+        (-295, 219,),
+        (),
+        (167, 258,),
+        (),
+    ),
+    (1, 3): (
+        (-310, -2, -79, -170, -261, -11, -88, -179, -266, -47, -132, -223, -290, -309, -1, -23, 310, 2, 79,
+         -78, 170, -100, 261, 11, 88, 179, 266, 47, 132, 223, 290, -5, 311, 3, 7, -169, 80, 84, 29, -260, -14,
+         171, -58, -191, 175, 309, 110, -311, -10, 262, -274, 264, 1, 201, 4, -3, -6, -7, -87, 12, 16, 78, 66,
+         -80, -83, -178, 155, -265, 93, 246, -48, 89, -101, 184, -35, 180, 269, 229, -116, 267, 81, -84, 169,
+         -171, -174, 32, 273, -192, 294, 292, 172, -175, 260, 113, -262, -275, 204, 263, -264, 24, 10, -29,
+         -12, -15, -207, 13, -16, 87, -30, -89, -92, -117, 25, -32, 178, -33, -180, -183, -208, 90, -93, 102,
+         -110, -111, 271, 265, -267, 181, -184, -282, 268, -269, -283, 193, 98, 96, -97, -201, -202, -99, 52,
+         -53, -56, 189, -21, -190, 43, 62, -66, 187, -188, -141, 151, -155, 270, -271, -232,),
+        (272, 133, 137, 128, -98, -273, -134, -138, -142,),
+        (242, 224, 228, 67, 291, 293, -161, -225, -229, -246, -292, -294,),
+        (-159, -252, -189,),
+        (46,),
+        (157, -158, -250, -272, 131, 219, 63, -67, 248, -249, -54, 42, -43,),
+        (222, 156, 247, 45, 127, -46, -128, -64,),
+        (218, -219,),
+        (-139,),
+        (304, 76, -230, -233, -297, -295, -298, 163, -167, 254, -258,),
+        (),
+    ),
+    (2, 0): (
+        (-309, -310, -1, -2, -24, -78, -79, -102, -169, -170, -193, -260, -261, -263, -10, -11, -88, -179,
+         -266, -268, -47, -62, -132, -151, -223, -242, -290, -293, 310, 2, 79, 170, -87, 261, -36, 11, 88,
+         179, 266, 47, 132, 309, -311, 223, -178, -118, 290, 1, -3, -265, 5, -8, -25, 78, -80, -291, 82, -85,
+         -103, 23, -19, -26, -27, 169, -171, 173, -176, -194, 100, -96, -104, -105, -209, 260, -262, 14, -17,
+         191, -187, -195, -196, 10, -12, 91, -94, 274, -270, -276, -277, -37, 311, 182, -185, 3, 8, 87, -89,
+         58, -59, -119, 80, 178, -180, 26, -60, 265, -267, 104, -210, 85, 48, -49, -50, 6, -9, 176, 133, -134,
+         -135, 83, -86, 224, 56, -57, -63, -225, -226, 275, -279, -280, 174, -177, 15, -18, 17, 171, 147, 195,
+         -148, 141, -143, 262, 39, -40, -149, 92, 276, -95, 232, -234, 12, 183, -186, 297, -299, -301, -152,
+         121, -122, 9, 89, -243, 212, -213, 107, 94, 285, -286, 238, -239, 185, 198, 180, 59, -240, 279,),
+        (267, 148, -68, -73, -74,),
+        (18, 40, 49, 239,),
+        (122, 71, -72,),
+        (162, 288, -303, -289, 253, 125, 213, 57, 298, -300, 143, 216, 234, 286, 144, 70, -75, 289,),
+        (),
+        (),
+        (),
+        (165, 256, 305, -306, -307, 235, 299, 300,),
+        (),
+        (),
+    ),
+    (2, 1): (
+        (-310, -2, -79, -81, -170, -172, -261, -263, -11, -88, -179, -266, -90, -47, -132, -223, -290, -181,
+         -309, -1, 310, 2, 79, -268, 170, 261, 11, 88, 179, 266, 47, 132, -137, 223, 290, -228, 311, -293, 3,
+         8, 80, 85, 26, 171, -24, 176, 309, -311, 104, 262, 17, 1, -3, 5, 195, -8, -19, -78, 12, -25, 94, 78,
+         -80, 276, -102, 23, -26, -27, -96, 100, -104, -105, 185, 82, -85, -193, 89, 59, -169, 173, -176, 180,
+         -62, -260, 267, -151, -10, 49, 9, 14, -17, 169, -171, -187, -87, -242, 134, 86, 191, -195, 57, 225,
+         260, 279, -196, -262, -270, -36, 274, -276, 177, 10, -277, -12, -37, -118, 18, -178, 6, -9, -209,
+         148, 87, -89, 143, 40, 95, 101, -107, -108, 91, 234, -94, -265, 186, 182, 299, -185, -133, 122, -224,
+         213, 178, 192, 58, -198, -199, -180, -59, 286, 239, 265, 275, 147, -279, -280, -267, -148,),
+        (48, 238, 15, 39, -18, -40, -49, -50, -60, -63, -239,),
+        (121, -157, -122, -149,),
+        (161, -162, -163, -248, -240, -291,),
+        (212, 56, 124, 252, -164, -253, -125, -213, -57, -254, 141, -143, -145, 72, 215, -216, 232, -234,
+         -236, 285, -286, 289, -255, 142, -144, 288, -289,),
+        (300,),
+        (),
+        (75,),
+        (159, -160, -165, 250, -251, -256, 233, -235, 307, 297, -299, -301, 298, -300,),
+        (),
+        (),
+    ),
+    (2, 2): (
+        (-309, -310, -1, -2, -4, -78, -79, -81, -169, -170, -172, -260, -261, -263, -10, -11, -88, -179, -266,
+         -13, -47, -132, -223, -290, 310, 2, 79, 170, 261, 11, 88, 179, 266, 47, 132, 309, -311, 223, -87,
+         -90, 290, 1, -3, -178, -181, 5, -8, 78, -80, -265, -268, 82, -85, 173, -176, 169, -171, -48, 14, -17,
+         260, -262, -133, 91, -94, 10, -12, -224, 182, -270, -185, 58, -59, 311, 87, -89, 147, -148, 35, -38,
+         3, 238, -228, -239, 178, -180, -39, 265, -267, 6, -9, -293, 291, -292, 8, 83, -86, 116, -120, 27,
+         -28, -121, 174, -177, 207, -211, 105, -106, -212, 282, -284, 196, -197, -285, 15, 17, -18, 277, -278,
+         59, 92, -95, 9, 80, 183, -186, 60, -61, 28, 106, 86, 171, 177, 280, -281, 262, 18, 12, 95, 38, 186,
+         120, 89, 149, -150, 197, 278, 283, -287, -288, 301, -302, 211, 123, 180, 109, 214, 267, 284, 134,
+         287, 225, 240, -241, 200, 281,),
+        (),
+        (),
+        (162, 71, 61, 150, -72,),
+        (241, -303,),
+        (146, 292,),
+        (253, 237,),
+        (),
+        (166, 257, 306, -308, 302,),
+        (),
+        (),
+    ),
+    (2, 3): (
+        (-310, -2, -79, -170, -261, -11, -88, -179, -266, -47, -132, -223, -290, -309, -1, -4, 310, 2, 79,
+         170, -78, -81, 261, 11, 88, 179, 266, 47, 132, 223, 290, 311, 3, 8, -172, 80, 85, 176, -263, 171,
+         309, -311, 17, -169, 262, -13, 1, -3, 94, -260, 12, -90, 185, -10, 59, 5, -8, -181, 89, 148, 38, 239,
+         -87, 180, -268, 267, 9, 292, -52, 14, -17, -137, 86, 120, 28, 58, -59, -228, 177, 211, 106, -178,
+         -293, 284, 197, 6, -9, 78, -80, -265, -96, 18, 278, 27, -28, -48, 105, -106, 95, 83, -86, 186, 169,
+         -171, -187, 174, -177, 61, 260, -262, -270, 15, -18, 10, -12, 92, -95, 35, -38, -39, 183, -186, 116,
+         -120, -121, 87, -89, 281, 196, -197, 277, -278, 207, -211, -212, 117, -123, -124, 178, -180, 150,
+         108, -109, 208, -214, -215, 287, 265, 302, -267, 282, -284, -285, 133, -134, 283, -287, -288, 224,
+         -225, 199, -200, 280, -281,),
+        (),
+        (60, 161, 241, 149, -157, -162, -61, -150,),
+        (240, -248, -241,),
+        (291, 145, -146, -292,),
+        (236, 252, -253, -237,),
+        (72,),
+        (),
+        (160, -166, 251, -257, 301, -302,),
+        (308,),
+        (),
+    ),
+}
+
+
+def kernel(panels, root_hbm, inverse_hbm, hamilton_hbm, margin_hbm, hamilton_mask_hbm,
            root_out, inverse_out, lowdin_out,
-           root, inverse, hamilton, poly, margin, next_rows, send_sem, recv_sem):
+           root, inverse, hamilton, poly, margin, next_rows, root_in, inverse_in, hamilton_in,
+           margin_in, hamilton_mask_in, load_sem, send_sem, recv_sem):
     cannon, rep = lax.axis_index("cannon"), lax.axis_index("rep")
     refs = {"R": root, "I": inverse, "H": hamilton, "P": poly, "M": margin}
     ahead, behind = lax.rem(cannon + 1, panels), lax.rem(cannon + panels - 1, panels)
@@ -255,6 +503,13 @@
     far = ((place == Z_PANELS - 1) & (rep >= 2)) | ((place == 0) & (rep < 2))
     beyond = lax.rem(cannon + jnp.where(place == 0, panels - 1, 1), panels)
 
+    loads = [pltpu.make_async_copy(source, target, load_sem.at[n]) for n, (source, target) in enumerate((
+        (margin_hbm, margin_in), (root_hbm, root_in), (inverse_hbm, inverse_in),
+        (hamilton_mask_hbm, hamilton_mask_in), (hamilton_hbm, hamilton_in),
+    ))]
+    for load in loads:
+        load.start()
+
     barrier = pltpu.get_barrier_semaphore()
     for peer in ((ahead, rep), (behind, rep), (cannon, sibling), (cannon, across)):
         pl.semaphore_signal(barrier, inc=1, device_id=peer, device_id_type=MESH)
@@ -263,6 +518,17 @@
     def _():
         pl.semaphore_signal(barrier, inc=1, device_id=(beyond, across), device_id_type=MESH)
 
+    for array in (root, inverse, hamilton, poly):
+        for row in range(SPAN):
+            right = row + HALF
+            if right < SPAN:
+                array[row * BLK:(row + 1) * BLK, right * BLK:] = jnp.zeros((BLK, (SPAN - right) * BLK), jnp.bfloat16)
+            left = row - HALF
+            if left > 0:
+                array[row * BLK:(row + 1) * BLK, :left * BLK] = jnp.zeros((BLK, left * BLK), jnp.bfloat16)
+
+    for load in loads:
+        load.wait()
     for array, source, scale in (
         (root, root_in, margin_in), (inverse, inverse_in, margin_in), (hamilton, hamilton_in, hamilton_mask_in),
     ):
@@ -275,15 +541,6 @@
         for b in range(2):
             keep = margin_in[b, j].astype(jnp.float32)
             margin[pl.ds(rep * 8 + j * 2 + b, 1), :] = jnp.full((1, BLK), keep, jnp.float32)
-    for array in (root, inverse, hamilton, poly):
-        for row in range(SPAN):
-            right = row + HALF
-            if right < SPAN:
-                array[row * BLK:(row + 1) * BLK, right * BLK:] = jnp.zeros((BLK, (SPAN - right) * BLK), jnp.bfloat16)
-            left = row - HALF
-            if left > 0:
-                array[row * BLK:(row + 1) * BLK, :left * BLK] = jnp.zeros((BLK, left * BLK), jnp.bfloat16)
-
     @pl.when(far)
     def _():
         pl.semaphore_wait(barrier, 5)
@@ -300,33 +557,6 @@
                 def _():
                     plan(Role(kind, role, refs, send_sem, recv_sem, cannon, panels))
 
-    def gather(d):
-        d.send("R", "zo", "co")
-        d.send("R", "po", "mo", "Xpo", "Xmo")
-        d.send("M", "zo", "co")
-        d.send("I", "zo", "co")
-        d.pass_on("R", "zo", "cz", "pz", "mz", "Xpz", "Xmz")
-        d.send("I", "po", "mo", "Xpo", "Xmo")
-        d.pass_on("M", "zo", "cz")
-        d.pass_on("R", "po", "cpo")
-        d.pass_on("R", "mo", "cmo")
-        d.send("H", "zo", "co", "po", "mo", "Xpo", "Xmo", "Xml")
-        d.pass_on("I", "zo", "cz", "mz", "Xmz", "Xpz")
-        d.pass_on("R", "pz", "cpz")
-        d.pass_on("R", "mz", "cmz")
-        for end in ("po", "mo", "pz", "mz"):
-            d.pass_on("R", "X" + end, "Xz" + end, "Xc" + end)
-        d.pass_on("I", "po", "cpo", "zpo")
-        d.pass_on("H", "zo", "cz", "pz", "Xpz", "Xmz")
-        for end in ("po", "mo", "pz", "mz"):
-            d.pass_on("R", "Xz" + end, "Xcz" + end)
-        d.recv("M", "co", "cz")
-        d.recv("I", "co", "cz")
-        d.recv("R", "co", "cz", "cpo", "cpz", "cmo", "cmz")
-        for end in ("po", "mo", "pz", "mz"):
-            d.recv("R", "Xc" + end, "Xcz" + end)
-
-    by_role(gather)
 
     def mask_row(i):
         return jnp.concatenate([margin[(t // 2) * 8 + i * 2 + t % 2:(t // 2) * 8 + i * 2 + t % 2 + 1, :]
@@ -340,68 +570,32 @@
 
     at_row = lax.broadcasted_iota(jnp.int32, (BLK, NS * BLK), 0)
     at_col = lax.broadcasted_iota(jnp.int32, (BLK, NS * BLK), 1)
-    diagonal = jnp.where(at_col - HALF * BLK == at_row, 1.5, 0.0).astype(jnp.float32)
     for i in range(ROWS):
+        by_role(lambda d: d.play(i))
         product = jnp.dot(inverse[own(i), window(i)], root[window(i), window(i)], preferred_element_type=jnp.float32)
+        diagonal = jnp.where(at_col - HALF * BLK == at_row, 1.5, 0.0).astype(jnp.float32)
         poly[own(i), window(i)] = (diagonal - 0.5 * (product * mask_row(i))).astype(jnp.bfloat16)
 
-    def exchange(d):
-        d.send("P", "p", "m", "Xp", "Xq", "Xm", "Xn")
-        d.pass_on("I", "mo", "cmo")
-        d.pass_on("I", "mz", "cmz")
-        for end in ("po", "mo", "pz", "mz"):
-            d.pass_on("I", "X" + end, "Xz" + end, "Xc" + end)
-        d.pass_on("I", "zpo", "czpo")
-        d.pass_on("H", "po", "cpo", "zpo")
-        d.pass_on("H", "mo", "cmo", "zmo")
-        d.pass_on("H", "pz", "cpz")
-        for end in ("po", "mo", "pz", "mz"):
-            d.pass_on("I", "Xz" + end, "Xcz" + end)
-        d.recv("I", "cpo", "cmo", "cmz", "czpo")
-        for end in ("po", "mo", "pz", "mz"):
-            d.recv("I", "Xc" + end, "Xcz" + end)
-
-    by_role(exchange)
-
     for i in range(ROWS):
+        by_role(lambda d: d.play(ROWS + i))
         product = jnp.dot(poly[own(i), window(i)], inverse[window(i), window(i)], preferred_element_type=jnp.float32)
         next_rows[i] = (product * mask_row(i)).astype(jnp.bfloat16)
         mine = next_rows[i, :, pl.ds(pl.multiple_of(2 * rep * BLK, 2 * BLK), 2 * BLK)]
         for b in range(2):
             inverse_out[i, b] = mine[:, b * BLK:(b + 1) * BLK]
 
-    def settle(d):
-        d.pass_on("H", "zpo", "czpo")
-        d.pass_on("H", "zmo", "czmo")
-        d.pass_on("H", "Xpo", "Xzpo", "Xcpo")
-        d.pass_on("H", "Xpz", "Xcpz")
-        for end in ("mo", "mz", "ml"):
-            d.pass_on("H", "X" + end, "Xc" + end)
-        d.pass_on("H", "Xzpo", "Xczpo")
-        d.pass_on("P", "p", "cp")
-        d.pass_on("P", "m", "cm")
-        for end in ("q", "n", "p", "m"):
-            d.pass_on("P", "X" + end, "Xc" + end)
-        d.recv("H", "co", "cz", "cpo", "cpz", "cmo", "czpo", "czmo")
-        d.recv("H", "Xcpo", "Xcpz", "Xczpo", "Xcmo", "Xcmz", "Xcml")
-
-    by_role(settle)
-
     def narrow(first, second, i):
         cols = pl.ds(pl.multiple_of((i + 2 * rep) * BLK, BLK), 2 * BLK)
         return jnp.dot(first, second[window(i), cols], preferred_element_type=jnp.float32)
 
+    by_role(lambda d: d.play(2 * ROWS))
     for i in range(ROWS):
         product = narrow(next_rows[i], hamilton, i)
         for b in range(2):
             keep = hamilton_mask_in[b, i].astype(jnp.float32)
             lowdin_out[i, b] = (product[:, b * BLK:(b + 1) * BLK] * keep).astype(jnp.bfloat16)
 
-    def last(d):
-        d.recv("P", "cp", "cm", "Xcp", "Xcq", "Xcm", "Xcn")
-
-    by_role(last)
-
+    by_role(lambda d: d.play(2 * ROWS + 1))
     for i in range(ROWS):
         product = narrow(root[own(i), window(i)], poly, i)
         for b in range(2):
@@ -409,16 +603,29 @@
             root_out[i, b] = (product[:, b * BLK:(b + 1) * BLK] * keep).astype(jnp.bfloat16)
 
     def finish(d):
+        d.play(2 * ROWS + 2)
         d.drain()
 
     by_role(finish)
+
+
+def store(*refs):
+    held, arrived, left = refs[6:9], refs[9], refs[10]
+    inward = [pltpu.make_async_copy(refs[n], held[n], arrived.at[n]) for n in range(3)]
+    outward = [pltpu.make_async_copy(held[n], refs[3 + n], left.at[n]) for n in range(3)]
+    for copy in inward:
+        copy.start()
+    for n in range(3):
+        inward[n].wait()
+        outward[n].start()
+    for copy in outward:
+        copy.wait()
 
 
 def solution(mesh):
     panels = mesh.shape["cannon"]
     count = len(TABLE.rows)
     vmem = pl.BlockSpec(memory_space=pltpu.VMEM)
-    smem = pl.BlockSpec(memory_space=pltpu.SMEM)
 
     def body(root_margin, inverse_root, hamiltonian, margin_mask, hamilton_mask):
         shape = jax.ShapeDtypeStruct(root_margin.shape, jnp.bfloat16)
@@ -426,25 +633,40 @@
         def run(*refs):
             kernel(panels, *refs)
 
+        raw = pltpu.VMEM(root_margin.shape, jnp.bfloat16)
         band = pltpu.VMEM((SPAN * BLK, SPAN * BLK), jnp.bfloat16)
-        return pl.pallas_call(
+        results = pl.pallas_call(
             run,
             out_shape=(shape, shape, shape),
-            in_specs=[vmem, vmem, vmem, smem, smem],
+            in_specs=[pl.BlockSpec(memory_space=pltpu.HBM)] * 5,
             out_specs=(vmem, vmem, vmem),
             scratch_shapes=[
                 band, band, band, band,
                 pltpu.VMEM((4 * 8, BLK), jnp.float32),
                 pltpu.VMEM((ROWS, BLK, NS * BLK), jnp.bfloat16),
+                raw, raw, raw,
+                pltpu.SMEM((2, ROWS), jnp.int32),
+                pltpu.SMEM((2, ROWS), jnp.int32),
+                pltpu.SemaphoreType.DMA((5,)),
                 pltpu.SemaphoreType.DMA((count,)),
                 pltpu.SemaphoreType.DMA((count,)),
             ],
             compiler_params=pltpu.CompilerParams(
-                collective_id=0, has_side_effects=True, vmem_limit_bytes=48 << 20
+                collective_id=0, has_side_effects=True, vmem_limit_bytes=60 << 20
             ),
             cost_estimate=pl.CostEstimate(flops=4 * 4 * 268435456, bytes_accessed=6 * 262144, transcendentals=0),
             name="newton_step",
         )(root_margin, inverse_root, hamiltonian, margin_mask.T, hamilton_mask.T)
+        there = pl.BlockSpec(memory_space=pl.ANY)
+        return pl.pallas_call(
+            store,
+            out_shape=(shape, shape, shape),
+            in_specs=[there] * 3,
+            out_specs=(there,) * 3,
+            scratch_shapes=[raw, raw, raw, pltpu.SemaphoreType.DMA((3,)), pltpu.SemaphoreType.DMA((3,))],
+            compiler_params=pltpu.CompilerParams(vmem_limit_bytes=60 << 20),
+            name="store",
+        )(*results)
 
     spec = P("cannon", "rep", None, None)
     mask = P("cannon", "rep")

time: 69.8 us -> 65.8 us (0.943)
  local copies, waits for them, and re-layouts: 5.64 us -> 0 us
  Pallas kernels: 62.8 us -> 64.3 us
    unnamed x13 -> x0, local copies, waits for them, and re-layouts: 5.64 us -> none
    pallas_call x1 -> x2, Pallas kernels: 62.8 us -> 64.3 us  [the longest x1 62.4 us: body(): pl.pallas_call(run, out_shape=(shape, shape, shape), in_specs=[pl.BlockSp...]
where the time goes in v3:
time: 65.8 us; the launch traced here: 65.1 us
  Pallas kernels  64.3 us (98%)
  between operations  0.8 us (1%)
    pallas_call x1, Pallas kernels, body(): pl.pallas_call(run, out_shape=(shape, shape, shape), in_specs=[pl.BlockSp...  62.4 us
    pallas_call x1, Pallas kernels, body(): pl.pallas_call(store, out_shape=(shape, shape, shape), in_specs=[there] *...  1.88 us

profile of v3, /device:TPU:1, one launch (start us, length us, event | category | flops | bytes accessed | tf_op | source)
XLA Modules:
  0.0 65.1 jit_solution(17467118033299189590)
XLA Ops:
  0.6 62.4 %newton_step.1 = (bf16[4,2,128,128]{3,2,1,0:T(8,128)(2,1)}, bf16[4,2,128,128]{3,2,1,0:T(8,128)(2,1)}, bf16[4,2,128,128]{3,2,1,0:T(8,128)(2,1)}) custom-call(bf16[4,2,128,128]{3,2,1,0:T(8,128)(2,1)} %refs_0_.1, bf16[4,2,128,128]{3,2,1,0:T(8,128)(2,1)} %refs_1_.1, bf16[4,2,128,128]{3,2,1,0:T(8,128)(2,1)} %refs_2_.1, s32[2,4]{1,0:T(2,128)} %bitcast.2, ...), custom_call_target="tpu_custom_call" | custom-call | flops 4294967296 | bytes 1572864 | tf_op jit(solution)/shard_map/newton_step/pallas_call | solution.py:638
  63.1 1.9 %store.1 = (bf16[4,2,128,128]{3,2,1,0:T(8,128)(2,1)}, bf16[4,2,128,128]{3,2,1,0:T(8,128)(2,1)}, bf16[4,2,128,128]{3,2,1,0:T(8,128)(2,1)}) custom-call(bf16[4,2,128,128]{3,2,1,0:T(8,128)(2,1)} %get-tuple-element.6.refs_0_, bf16[4,2,128,128]{3,2,1,0:T(8,128)(2,1)} %get-tuple-element.7.refs_1_, bf16[4,2,128,128]{3,2,1,0:T(8,128)(2,1)} %get-tuple-element.8.refs_2_), custom_call_target="tpu_custom_call" | custom-call | tf_op jit(solution)/shard_map/store/pallas_call | solution.py:661
